TPU v7x, 32 devices: a whole 2x2x4 slice. The times are simulated.
32 devices in a mesh: groups: 2 (over x), dp: 16 (over z, y, core).
Axes of the slice: x: 2, y: 2, z: 4, core: 2. Of those that a mesh axis runs over, the one named last changes fastest.
Arguments:
- tokens: bfloat16 [4096, 5120], P(('groups', 'dp')), parts along dimension 0, may hold values from -6 to 6
- cotangent: bfloat16 [4096, 5120], P(('groups', 'dp')), parts along dimension 0, may hold values from -6 to 6
- segments: int32 [32, 1, 3], P('groups'), parts along dimension 0, may hold values from 0 to 15, as said below
- owner_map: int32 [32], P('groups'), parts along dimension 0, may hold values from 0 to 15, each once
- down_t: bfloat16 [32, 64, 5120], P(('groups', 'dp')), parts along dimension 0, may hold values from -0.078125 to 0.078125
- up: bfloat16 [32, 64, 5120], P(('groups', 'dp')), parts along dimension 0, may hold values from -0.75 to 0.75
Outputs:
- grad_tokens: bfloat16 [4096, 5120], P(('groups', 'dp')), parts along dimension 0
- grad_down: bfloat16 [32, 64, 5120], P(('groups', 'dp')), parts along dimension 0
- grad_up: bfloat16 [32, 64, 5120], P(('groups', 'dp')), parts along dimension 0
There are 2 independent parts, one for each index of `groups`. A program takes and returns all parts, laid end to end along the dimension named above; each array names one. Nothing has to cross between parts.
Inputs may be any that keep to these rules, and one draw needn't show every extreme that they name: In segments[d] the live entries (count 1 or more) come first, cover blocks 0 to 0 in order without gaps, and the rest are (0, 0, 0); ids name adapters, some far more often than others.
All inputs are finite; a program needn't handle non-finite values.
Results may differ from a plain program's by a relative error of at most 0.0075.
Values may be sent and summed in bfloat16 or wider, within the bound.
No kernel may reach another device: no remote copies, remote signals or barrier semaphores. Data moves between devices by JAX's collectives and lax.ppermute only.
A program may use at most 64 MiB of HBM per device.

v0:
```python
import functools

import jax
import jax.numpy as jnp
from jax import lax
from jax.experimental import pallas as pl
from jax.experimental.pallas import tpu as pltpu
from jax.sharding import PartitionSpec as P

BLOCK = 128
F32 = jnp.float32
BF16 = jnp.bfloat16
I32 = jnp.int32
VMEM = pl.BlockSpec(memory_space=pltpu.VMEM)
SMEM = pl.BlockSpec(memory_space=pltpu.SMEM)


def block_slots(segments, owner_map, blocks, count_adapters):
    index = jnp.arange(blocks, dtype=I32)
    ids = segments[:, :, 0]
    starts = segments[:, :, 1]
    counts = segments[:, :, 2]
    inside = (index[None, None, :] >= starts[:, :, None]) & (
        index[None, None, :] < (starts + counts)[:, :, None]
    )
    adapter = jnp.sum(jnp.where(inside, ids[:, :, None], 0), axis=1)
    match = adapter[:, :, None] == jnp.arange(count_adapters, dtype=I32)[None, None, :]
    slots = jnp.sum(jnp.where(match, owner_map[None, None, :], 0), axis=2)
    return slots.reshape(-1)


def dot(spec, a, b):
    return jnp.einsum(spec, a, b, preferred_element_type=F32)


def two_step(slots, tokens, cotangent, down_t, up):
    devices = lax.axis_size("dp")
    rank, width = down_t.shape[1:]
    piece = 2 * rank // devices
    exchange = functools.partial(
        lax.all_to_all, axis_name="dp", split_axis=0, concat_axis=0, tiled=True
    )
    stack = jnp.concatenate([down_t[0], up[0]], axis=0).reshape(devices, piece, width)
    table = exchange(stack)
    mine = exchange(jnp.take(table, slots, axis=0, mode="clip")).reshape(2 * rank, width)
    down, up_ = mine[:rank], mine[rank:]
    hidden = dot("td,rd->tr", tokens, down).astype(BF16)
    inner = dot("td,rd->tr", cotangent, up_).astype(BF16)
    grad_rows = dot("tr,rd->td", inner, down).astype(BF16)
    terms = jnp.concatenate(
        [dot("tr,td->rd", inner, tokens), dot("tr,td->rd", hidden, cotangent)], axis=0
    ).astype(BF16)
    pieces = exchange(terms.reshape(devices, piece, width))
    onehot = (slots[None, :] == jnp.arange(devices, dtype=I32)[:, None]).astype(BF16)
    summed = dot("kb,bpd->kpd", onehot, pieces) * (1.0 / BLOCK)
    grads = exchange(summed.astype(BF16)).reshape(2, rank, width)
    return grad_rows, grads[:1], grads[1:]


STEPS = ((0, 0), (1, 1), (2, 4), (4, 2), (6, 6), (3, 5), (5, 3), (7, 7))


def partners(sending):
    own = lax.rem(lax.axis_index("dp"), len(STEPS))
    places = []
    for a, b in STEPS:
        if a % 2 and not sending:
            a, b = b, a
        places.append(own ^ jnp.where(own % 2 == 1, b, a) if a != b else own ^ a)
    return places


def call(kernel, scalars, arrays, outs, scratch=(), after=()):
    size = 4 << 20
    for array in list(arrays) + list(outs) + list(scratch):
        extent = array.dtype.itemsize
        for value in array.shape:
            extent *= value
        size += extent
    given = len(scalars) + len(arrays)
    return pl.pallas_call(
        lambda *refs: kernel(*refs[:given], *refs[given + len(after) :]),
        out_shape=outs,
        in_specs=[SMEM] * len(scalars)
        + [VMEM] * len(arrays)
        + [pl.BlockSpec(memory_space=pl.ANY)] * len(after),
        out_specs=[VMEM] * len(outs),
        scratch_shapes=[pltpu.VMEM(s.shape, s.dtype) for s in scratch],
        compiler_params=pltpu.CompilerParams(vmem_limit_bytes=size),
    )(*scalars, *arrays, *after)


SEND, ARRIVED, FETCH, CROSS, LOCAL = range(5)


def routes(segments, owner_map, devices, capacities):
    half = devices // 2
    entries = segments.shape[1]

    def kernel(segments_ref, owner_ref, out_ref, branch_ref, slot_ref, need_ref, place_ref):
        side = lax.div(lax.axis_index("dp"), half)
        for d in range(devices):
            need_ref[d] = 0
            adapter = 0
            for e in range(entries):
                start = segments_ref[1, e, d]
                inside = (start <= 0) & (start + segments_ref[2, e, d] > 0)
                adapter += jnp.where(inside, segments_ref[0, e, d], 0)
            slot_ref[d] = owner_ref[adapter]
        for d in range(devices):
            slot = slot_ref[d]
            need_ref[slot] = jnp.where(lax.div(slot, half) != d // half, 1, need_ref[slot])
        for j in range(half):
            out_ref[SEND, j] = 0
            out_ref[ARRIVED, j] = half
        counts = []
        for s in range(2):
            count = jnp.int32(0)
            for k in range(half):
                needed = need_ref[s * half + k]
                place_ref[s * half + k] = count

                @pl.when((side == s) & (needed == 1))
                def _(count=count, k=k):
                    out_ref[SEND, count] = k
                    out_ref[ARRIVED, count] = k

                count += needed
            counts.append(count)
        most = jnp.maximum(counts[0], counts[1])
        branch = jnp.int32(0)
        for capacity in capacities[:-1]:
            branch += jnp.where(most > capacity, 1, 0)
        branch_ref[0] = branch
        for u in range(half):
            slot = slot_ref[side * half + u]
            local = lax.div(slot, half) == side
            place = place_ref[slot]
            k = lax.rem(slot, half)
            out_ref[FETCH, u] = jnp.where(local, k, half + place)
            out_ref[CROSS, u] = jnp.where(local, half, place)
            out_ref[LOCAL, u] = jnp.where(local, k, half)

    return pl.pallas_call(
        kernel,
        out_shape=[jax.ShapeDtypeStruct((5, half), I32), jax.ShapeDtypeStruct((1,), I32)],
        in_specs=[SMEM] * 2,
        out_specs=[SMEM] * 2,
        scratch_shapes=[pltpu.SMEM((devices,), I32)] * 3,
    )(jnp.transpose(segments, (2, 1, 0)), owner_map)


def split_pieces(stacked, after=()):
    half = stacked.shape[0]

    def kernel(stacked_ref, *out_refs):
        for ref, p in zip(out_refs, partners(True)):
            ref[...] = stacked_ref[p]

    piece = jax.ShapeDtypeStruct(stacked.shape[1:], BF16)
    return call(kernel, [], [stacked], [piece] * half, after=after)


def join_pieces(pieces):
    half = len(pieces)

    def kernel(*refs):
        for ref, p in zip(refs, partners(False)):
            refs[half][p] = ref[...]

    out = jax.ShapeDtypeStruct((half,) + pieces[0].shape, BF16)
    return call(kernel, [], pieces, [out])[0]


def pick_crossing(route, table, count, after=()):
    half = len(table)
    shape = table[0].shape

    def kernel(route_ref, *refs):
        out_ref, all_ref = refs[half:]
        for ref, p in zip(refs, partners(False)):
            all_ref[p] = ref[...]
        for j in range(count):
            out_ref[j] = all_ref[route_ref[SEND, j]]

    out = jax.ShapeDtypeStruct((count,) + shape, BF16)
    scratch = jax.ShapeDtypeStruct((half,) + shape, BF16)
    return call(kernel, [route], table, [out], [scratch], after)[0]


def pick_pieces(route, table, arrived, terms=None, after=()):
    half = len(table)
    count = arrived.shape[0]
    shape = table[0].shape
    arrays = list(table) + [arrived] + ([] if terms is None else [terms])

    def kernel(route_ref, *refs):
        out_refs, all_ref = refs[len(arrays) : -1], refs[-1]
        for ref, p in zip(refs[:half], partners(False)):
            all_ref[p] = ref[...]
        for j in range(count):
            all_ref[half + j] = refs[half][j]
        for ref, p in zip(out_refs, partners(True)):
            if terms is None:
                ref[...] = all_ref[route_ref[FETCH, p]]
            else:
                ref[0] = all_ref[route_ref[FETCH, p]]
                ref[1] = refs[half + 1][p]

    out = jax.ShapeDtypeStruct(shape if terms is None else (2,) + shape, BF16)
    scratch = jax.ShapeDtypeStruct((half + count,) + shape, BF16)
    return call(kernel, [route], arrays, [out] * half, [scratch], after)


def lower(ref):
    return ref[1] if len(ref.shape) == 3 else ref[...]


def upper(ref):
    return ref[0] if len(ref.shape) == 3 else ref[...]


def sum_crossing(route, pieces, count, after=()):
    half = len(pieces)
    shape = pieces[0].shape[-2:]

    def kernel(route_ref, *refs):
        out_ref, total_ref = refs[half:]
        total_ref[...] = jnp.zeros_like(total_ref)
        for ref, p in zip(refs[:half], partners(False)):
            place = route_ref[CROSS, p]
            total_ref[place] = total_ref[place] + lower(ref).astype(F32)
        for k in range(count):
            out_ref[k] = total_ref[k].astype(BF16)

    out = jax.ShapeDtypeStruct((count,) + shape, BF16)
    scratch = jax.ShapeDtypeStruct((half + 1,) + shape, F32)
    return call(kernel, [route], pieces, [out], [scratch], after)[0]


def sum_pieces(route, pieces, arrived, after=()):
    half = len(pieces)
    count = arrived.shape[0]
    shape = pieces[0].shape[-2:]

    def kernel(route_ref, *refs):
        out_refs, total_ref = refs[half + 1 : -1], refs[-1]
        total_ref[...] = jnp.zeros_like(total_ref)
        for ref, p in zip(refs[:half], partners(False)):
            place = route_ref[LOCAL, p]
            total_ref[place] = total_ref[place] + lower(ref).astype(F32)
        for j in range(count):
            place = route_ref[ARRIVED, j]
            total_ref[place] = total_ref[place] + refs[half][j].astype(F32)
        for ref, p in zip(out_refs, partners(True)):
            ref[...] = (total_ref[p] * (1.0 / BLOCK)).astype(BF16)

    out = jax.ShapeDtypeStruct(shape, BF16)
    scratch = jax.ShapeDtypeStruct((half + 1,) + shape, F32)
    arrays = list(pieces) + [arrived]
    return call(kernel, [route], arrays, [out] * half, [scratch], after)


def term_pieces(pieces, first, second, whole, after=()):
    half = len(pieces)
    rows, width = first.shape
    piece = pieces[0].shape[-2]
    rank = half * piece
    step = max(s for s in (128, 256, 512, 640, 1024) if width % s == 0)

    def kernel(*refs):
        first_ref, second_ref = refs[half : half + 2]
        if whole:
            adapter_ref, term_ref = refs[half + 2 :]
        else:
            projected_ref, out_refs = refs[half + 2], refs[half + 3 : -2]
            adapter_ref, term_ref = refs[-2:]
        for ref, p in zip(refs[:half], partners(False)):
            adapter_ref[p] = upper(ref)
        total = jnp.zeros((rows, rank), F32)
        for low in range(0, width, step):
            total += lax.dot_general(
                first_ref[:, low : low + step],
                adapter_ref[:, :, low : low + step].reshape(rank, step),
                (((1,), (1,)), ((), ())),
                preferred_element_type=F32,
            )
        if not whole:
            projected_ref[...] = total.astype(BF16)
        turned = total.T.astype(BF16)
        for low in range(0, width, step):
            term = jnp.dot(turned, second_ref[:, low : low + step], preferred_element_type=F32)
            term_ref[:, :, low : low + step] = term.astype(BF16).reshape(half, piece, step)
        if not whole:
            for ref, p in zip(out_refs, partners(True)):
                ref[...] = term_ref[p]

    stacked = jax.ShapeDtypeStruct((half, piece, width), BF16)
    out = jax.ShapeDtypeStruct((piece, width), BF16)
    projected = jax.ShapeDtypeStruct((rows, rank), BF16)
    arrays = list(pieces) + [first, second]
    if whole:
        adapter, term = call(kernel, [], arrays, [stacked, stacked], after=after)
        return adapter.reshape(rank, width), term
    got = call(
        kernel, [], arrays, [projected] + [out] * half, [stacked, stacked], after
    )
    return got[0], got[1:]


def three_step(capacity, route, tokens, cotangent, table_down, up):
    devices = lax.axis_size("dp")
    half = devices // 2
    pairs = [(i, (i + half) % devices) for i in range(devices)]

    def across(array):
        return lax.ppermute(array, "dp", pairs)

    crossing_down = pick_crossing(route, table_down, capacity)
    arrived_down = across(crossing_down)
    table_up = exchange(split_pieces(up, [crossing_down]))
    crossing_up = pick_crossing(route, table_up, capacity, [arrived_down])
    arrived_up = across(crossing_up)
    got_down = exchange(pick_pieces(route, table_down, arrived_down, after=[crossing_up]))
    down, term_up = term_pieces(got_down, tokens, cotangent, True)
    got_both = exchange(pick_pieces(route, table_up, arrived_up, term_up))
    crossing_sums_up = sum_crossing(route, got_both, capacity)
    sums_up = across(crossing_sums_up)
    inner, term_down = term_pieces(got_both, cotangent, tokens, False, [crossing_sums_up])
    pieces_down = exchange(term_down)
    crossing_sums_down = sum_crossing(route, pieces_down, capacity, [sums_up])
    sums_down = across(crossing_sums_down)
    grad_up = exchange(sum_pieces(route, got_both, sums_up, [crossing_sums_down]))
    grad_rows = dot("tr,rd->td", inner, down).astype(BF16)
    return grad_rows, sum_pieces(route, pieces_down, sums_down), grad_up


def exchange(pieces):
    devices = lax.axis_size("dp")
    got = [pieces[0]]
    for piece, step in zip(pieces[1:], STEPS[1:]):
        got.append(lax.ppermute(piece, "dp", [(i, i ^ step[i % 2]) for i in range(devices)]))
    return got


def shards(tokens, cotangent, segments, owner_map, down_t, up):
    devices = lax.axis_size("dp")
    if devices != 2 * len(STEPS):
        slots = block_slots(segments, owner_map, 1, devices)
        return two_step(slots, tokens, cotangent, down_t, up)
    half = devices // 2
    rank, width = down_t.shape[1:]
    shape = (half, rank // half, width)
    capacities = [3, 4, 5, half]
    route, branch = routes(segments, owner_map, devices, capacities)
    table_down = exchange(split_pieces(down_t.reshape(shape)))
    grad_rows, grad_down, grad_up = lax.switch(
        branch[0],
        [functools.partial(three_step, c) for c in capacities],
        route,
        tokens,
        cotangent,
        table_down,
        up.reshape(shape),
    )
    grad_down = exchange(grad_down)
    return (
        grad_rows,
        join_pieces(grad_down).reshape(1, rank, width),
        join_pieces(grad_up).reshape(1, rank, width),
    )


def solution(mesh):
    in_specs = (
        P(("groups", "dp"), None),
        P(("groups", "dp"), None),
        P("groups", None, None),
        P("groups"),
        P(("groups", "dp"), None, None),
        P(("groups", "dp"), None, None),
    )
    out_specs = (
        P(("groups", "dp"), None),
        P(("groups", "dp"), None, None),
        P(("groups", "dp"), None, None),
    )
    return jax.shard_map(shards, mesh=mesh, in_specs=in_specs, out_specs=out_specs, check_vma=False)
```

profile of v0, /device:TPU:0, one launch (start us, length us, event | category | flops | bytes accessed | tf_op | source)
XLA Modules:
  0.0 132.4 jit_solution(16716661994057248043)
XLA Ops:
  0.6 1.1 copy-done
  2.3 2.6 %collective-permute-start.157 = (bf16[8,5120]{1,0:T(8,128)(2,1)S(1)}, bf16[8,5120]{1,0:T(8,128)(2,1)S(1)}, u32[]{:S(2)}, u32[]{:S(2)}) collective-permute-start(bf16[8,5120]{1,0:T(8,128)(2,1)S(1)} %get-tuple-element.400), channel_id=1, source_target_pairs={{0,2},{1,5},{2,0},{3,7},{4,6},{5,1},{6,4},{7,3},{8,10},{9,13},{10,... | collective-permute-start | bytes 245768 | tf_op jit(solution)/shard_map/ppermute | solution.py:342
  4.9 1.6 %collective-permute-start.158 = (bf16[8,5120]{1,0:T(8,128)(2,1)S(1)}, bf16[8,5120]{1,0:T(8,128)(2,1)S(1)}, u32[]{:S(2)}, u32[]{:S(2)}) collective-permute-start(bf16[8,5120]{1,0:T(8,128)(2,1)S(1)} %get-tuple-element.401), channel_id=1, source_target_pairs={{0,4},{1,3},{2,6},{3,1},{4,0},{5,7},{6,2},{7,5},{8,12},{9,11},{10,... | collective-permute-start | bytes 245768 | tf_op jit(solution)/shard_map/ppermute | solution.py:342
  6.5 1.1 collective-permute-start.160
  7.6 0.6 collective-permute-start.161
  8.2 2.1 %collective-permute-start.162 = (bf16[8,5120]{1,0:T(8,128)(2,1)S(1)}, bf16[8,5120]{1,0:T(8,128)(2,1)S(1)}, u32[]{:S(2)}, u32[]{:S(2)}) collective-permute-start(bf16[8,5120]{1,0:T(8,128)(2,1)S(1)} %get-tuple-element.405), channel_id=1, source_target_pairs={{0,7},{1,6},{2,5},{3,4},{4,3},{5,2},{6,1},{7,0},{8,15},{9,14},{10,... | collective-permute-start | bytes 245768 | tf_op jit(solution)/shard_map/ppermute | solution.py:342
  10.3 1.6 %shard_map.85 = (s32[5,8]{1,0:T(8,128)S(1)}, s32[1]{0:T(128)}) custom-call(s32[3,1,16]{2,1,0:T(1,128)} %bitcast.29, s32[16]{0:T(128)} %owner_ref.1), custom_call_target="tpu_custom_call" | custom-call | tf_op jit(solution)/shard_map/pallas_call | solution.py:144
  12.7 1.5 %collective-permute-done.161 = bf16[8,5120]{1,0:T(8,128)(2,1)S(1)} collective-permute-done((bf16[8,5120]{1,0:T(8,128)(2,1)S(1)}, bf16[8,5120]{1,0:T(8,128)(2,1)S(1)}, u32[]{:S(2)}, u32[]{:S(2)}) %collective-permute-start.161) | collective-permute-done | bytes 81952 | tf_op jit(solution)/shard_map/ppermute | solution.py:342
  14.2 106.4 %conditional.2 = (bf16[128,5120]{1,0:T(8,128)(2,1)S(1)}, bf16[8,5120]{1,0:T(8,128)(2,1)S(1)}, bf16[8,5120]{1,0:T(8,128)(2,1)S(1)}, bf16[8,5120]{1,0:T(8,128)(2,1...) conditional(s32[]{:T(128)} %bitcast.5, (s32[5,8]{1,0:T(8,128)S(1)}, ...), branch_computations={%region_0.0_spmd, %region_1.0_spmd, %region_2.0_spmd, %region_3.0_... | conditional | flops 83886080 | bytes 39339764
  14.2 0.7 branch_1_fun.11.refs_1_
  14.9 2.7 %collective-permute-start.46 = (bf16[4,8,5120]{2,1,0:T(8,128)(2,1)S(1)}, bf16[4,8,5120]{2,1,0:T(8,128)(2,1)S(1)}, u32[]{:S(2)}, u32[]{:S(2)}) collective-permute-start(bf16[4,8,5120]{2,1,0:T(8,128)(2,1)S(1)} %branch_1_fun.11.refs_1_), channel_id=1, source_target_pairs={{0,8},{1,9},{2,10},{3,11},{4,12},{5,13},{6,14},{7,15},{8,0},{9,1},... | collective-permute-start | bytes 983048 | tf_op jit(solution)/shard_map/cond/branch_1_fun/ppermute | solution.py:317
  18.2 1.2 collective-permute-start.40
  19.4 1.3 collective-permute-start.41
  20.6 1.0 collective-permute-start.42
  22.1 1.2 collective-permute-done.40.refs_3_
  23.2 6.1 %collective-permute-start.44 = (bf16[8,5120]{1,0:T(8,128)(2,1)S(1)}, bf16[8,5120]{1,0:T(8,128)(2,1)S(1)}, u32[]{:S(2)}, u32[]{:S(2)}) collective-permute-start(bf16[8,5120]{1,0:T(8,128)(2,1)S(1)} %get-tuple-element.193), channel_id=1, source_target_pairs={{0,5},{1,2},{2,7},{3,0},{4,1},{5,6},{6,3},{7,4},{8,13},{9,10},{10,... | collective-permute-start | bytes 245768 | tf_op jit(solution)/shard_map/cond/branch_1_fun/ppermute | solution.py:342
  29.3 2.0 %collective-permute-done.44.refs_7_ = bf16[8,5120]{1,0:T(8,128)(2,1)S(1)} collective-permute-done((bf16[8,5120]{1,0:T(8,128)(2,1)S(1)}, bf16[8,5120]{1,0:T(8,128)(2,1)S(1)}, u32[]{:S(2)}, u32[]{:S(2)}) %collective-permute-start.44) | collective-permute-done | bytes 81952 | tf_op jit(solution)/shard_map/cond/branch_1_fun/ppermute | solution.py:342
  31.4 4.1 %collective-permute-done.45.refs_8_ = bf16[8,5120]{1,0:T(8,128)(2,1)S(1)} collective-permute-done((bf16[8,5120]{1,0:T(8,128)(2,1)S(1)}, bf16[8,5120]{1,0:T(8,128)(2,1)S(1)}, u32[]{:S(2)}, u32[]{:S(2)}) %collective-permute-start.45) | collective-permute-done | bytes 81952 | tf_op jit(solution)/shard_map/cond/branch_1_fun/ppermute | solution.py:342
  35.5 0.7 branch_1_fun.13.refs_10_
  36.2 1.5 %collective-permute-start.47 = (bf16[4,8,5120]{2,1,0:T(8,128)(2,1)S(1)}, bf16[4,8,5120]{2,1,0:T(8,128)(2,1)S(1)}, u32[]{:S(2)}, u32[]{:S(2)}) collective-permute-start(bf16[4,8,5120]{2,1,0:T(8,128)(2,1)S(1)} %branch_1_fun.13.refs_10_), channel_id=1, source_target_pairs={{0,8},{1,9},{2,10},{3,11},{4,12},{5,13},{6,14},{7,15},{8,0},{9,1},... | collective-permute-start | bytes 983048 | tf_op jit(solution)/shard_map/cond/branch_1_fun/ppermute | solution.py:317
  37.7 0.7 branch_1_fun.14
  38.8 3.2 %collective-permute-start.50 = (bf16[8,5120]{1,0:T(8,128)(2,1)S(1)}, bf16[8,5120]{1,0:T(8,128)(2,1)S(1)}, u32[]{:S(2)}, u32[]{:S(2)}) collective-permute-start(bf16[8,5120]{1,0:T(8,128)(2,1)S(1)} %get-tuple-element.198), channel_id=1, source_target_pairs={{0,4},{1,3},{2,6},{3,1},{4,0},{5,7},{6,2},{7,5},{8,12},{9,11},{10,... | collective-permute-start | bytes 245768 | tf_op jit(solution)/shard_map/cond/branch_1_fun/ppermute | solution.py:342
  42.1 0.6 collective-permute-start.52
  43.1 3.8 %collective-permute-start.53 = (bf16[8,5120]{1,0:T(8,128)(2,1)S(1)}, bf16[8,5120]{1,0:T(8,128)(2,1)S(1)}, u32[]{:S(2)}, u32[]{:S(2)}) collective-permute-start(bf16[8,5120]{1,0:T(8,128)(2,1)S(1)} %get-tuple-element.201), channel_id=1, source_target_pairs={{0,5},{1,2},{2,7},{3,0},{4,1},{5,6},{6,3},{7,4},{8,13},{9,10},{10,... | collective-permute-start | bytes 245768 | tf_op jit(solution)/shard_map/cond/branch_1_fun/ppermute | solution.py:342
  46.9 0.8 collective-permute-done.50.refs_3_
  47.7 1.0 collective-permute-start.54
  48.8 5.1 %collective-permute-done.52.refs_5_ = bf16[8,5120]{1,0:T(8,128)(2,1)S(1)} collective-permute-done((bf16[8,5120]{1,0:T(8,128)(2,1)S(1)}, bf16[8,5120]{1,0:T(8,128)(2,1)S(1)}, u32[]{:S(2)}, u32[]{:S(2)}) %collective-permute-start.52) | collective-permute-done | bytes 81952 | tf_op jit(solution)/shard_map/cond/branch_1_fun/ppermute | solution.py:342
  54.0 2.8 %collective-permute-done.54.refs_7_ = bf16[8,5120]{1,0:T(8,128)(2,1)S(1)} collective-permute-done((bf16[8,5120]{1,0:T(8,128)(2,1)S(1)}, bf16[8,5120]{1,0:T(8,128)(2,1)S(1)}, u32[]{:S(2)}, u32[]{:S(2)}) %collective-permute-start.54) | collective-permute-done | bytes 81952 | tf_op jit(solution)/shard_map/cond/branch_1_fun/ppermute | solution.py:342
  56.8 1.2 branch_1_fun.15
  58.0 0.8 branch_1_fun.16
  58.8 0.7 collective-permute-start.55
  59.9 3.0 %collective-permute-start.58 = (bf16[2,8,5120]{2,1,0:T(8,128)(2,1)S(1)}, bf16[2,8,5120]{2,1,0:T(8,128)(2,1)S(1)}, u32[]{:S(2)}, u32[]{:S(2)}) collective-permute-start(bf16[2,8,5120]{2,1,0:T(8,128)(2,1)S(1)} %get-tuple-element.210), channel_id=1, source_target_pairs={{0,6},{1,7},{2,4},{3,5},{4,2},{5,3},{6,0},{7,1},{8,14},{9,15},{10,... | collective-permute-start | bytes 491528 | tf_op jit(solution)/shard_map/cond/branch_1_fun/ppermute | solution.py:342
  62.9 1.7 %collective-permute-start.60 = (bf16[2,8,5120]{2,1,0:T(8,128)(2,1)S(1)}, bf16[2,8,5120]{2,1,0:T(8,128)(2,1)S(1)}, u32[]{:S(2)}, u32[]{:S(2)}) collective-permute-start(bf16[2,8,5120]{2,1,0:T(8,128)(2,1)S(1)} %get-tuple-element.212), channel_id=1, source_target_pairs={{0,5},{1,2},{2,7},{3,0},{4,1},{5,6},{6,3},{7,4},{8,13},{9,10},{10,... | collective-permute-start | bytes 491528 | tf_op jit(solution)/shard_map/cond/branch_1_fun/ppermute | solution.py:342
  64.7 3.8 %collective-permute-done.56.refs_3_.refs_2_ = bf16[2,8,5120]{2,1,0:T(8,128)(2,1)S(1)} collective-permute-done((bf16[2,8,5120]{2,1,0:T(8,128)(2,1)S(1)}, bf16[2,8,5120]{2,1,0:T(8,128)(2,1)S(1)}, u32[]{:S(2)}, u32[]{:S(2)}) %collective-permute-start.56) | collective-permute-done | bytes 163872 | tf_op jit(solution)/shard_map/cond/branch_1_fun/ppermute | solution.py:342
  68.4 2.5 %collective-permute-done.58.refs_5_.refs_4_ = bf16[2,8,5120]{2,1,0:T(8,128)(2,1)S(1)} collective-permute-done((bf16[2,8,5120]{2,1,0:T(8,128)(2,1)S(1)}, bf16[2,8,5120]{2,1,0:T(8,128)(2,1)S(1)}, u32[]{:S(2)}, u32[]{:S(2)}) %collective-permute-start.58) | collective-permute-done | bytes 163872 | tf_op jit(solution)/shard_map/cond/branch_1_fun/ppermute | solution.py:342
  71.2 0.7 collective-permute-done.60.refs_7_.refs_6_
  71.9 4.1 %collective-permute-done.61.refs_8_.refs_7_ = bf16[2,8,5120]{2,1,0:T(8,128)(2,1)S(1)} collective-permute-done((bf16[2,8,5120]{2,1,0:T(8,128)(2,1)S(1)}, bf16[2,8,5120]{2,1,0:T(8,128)(2,1)S(1)}, u32[]{:S(2)}, u32[]{:S(2)}) %collective-permute-start.61) | collective-permute-done | bytes 163872 | tf_op jit(solution)/shard_map/cond/branch_1_fun/ppermute | solution.py:342
  76.0 0.8 branch_1_fun.17.refs_10_
  76.9 1.2 branch_1_fun.18
  78.5 1.2 collective-permute-start.63
  79.7 1.5 %collective-permute-start.64 = (bf16[8,5120]{1,0:T(8,128)(2,1)S(1)}, bf16[8,5120]{1,0:T(8,128)(2,1)S(1)}, u32[]{:S(2)}, u32[]{:S(2)}) collective-permute-start(bf16[8,5120]{1,0:T(8,128)(2,1)S(1)} %get-tuple-element.219), channel_id=1, source_target_pairs={{0,4},{1,3},{2,6},{3,1},{4,0},{5,7},{6,2},{7,5},{8,12},{9,11},{10,... | collective-permute-start | bytes 245768 | tf_op jit(solution)/shard_map/cond/branch_1_fun/ppermute | solution.py:342
  81.2 0.8 collective-permute-start.65
  82.0 1.3 collective-permute-done.63.refs_3_
  83.3 4.9 %collective-permute-start.67 = (bf16[8,5120]{1,0:T(8,128)(2,1)S(1)}, bf16[8,5120]{1,0:T(8,128)(2,1)S(1)}, u32[]{:S(2)}, u32[]{:S(2)}) collective-permute-start(bf16[8,5120]{1,0:T(8,128)(2,1)S(1)} %get-tuple-element.222), channel_id=1, source_target_pairs={{0,5},{1,2},{2,7},{3,0},{4,1},{5,6},{6,3},{7,4},{8,13},{9,10},{10,... | collective-permute-start | bytes 245768 | tf_op jit(solution)/shard_map/cond/branch_1_fun/ppermute | solution.py:342
  88.2 1.0 collective-permute-start.68
  89.2 1.2 collective-permute-done.67.refs_7_
  90.4 6.4 %collective-permute-done.68.refs_8_ = bf16[8,5120]{1,0:T(8,128)(2,1)S(1)} collective-permute-done((bf16[8,5120]{1,0:T(8,128)(2,1)S(1)}, bf16[8,5120]{1,0:T(8,128)(2,1)S(1)}, u32[]{:S(2)}, u32[]{:S(2)}) %collective-permute-start.68) | collective-permute-done | bytes 81952 | tf_op jit(solution)/shard_map/cond/branch_1_fun/ppermute | solution.py:342
  96.9 0.8 branch_1_fun.19.refs_10_
  97.8 1.0 branch_1_fun.21
  98.8 0.7 collective-permute-start.71
  99.5 0.9 collective-permute-start.72
  100.4 2.0 %collective-permute-start.73 = (bf16[8,5120]{1,0:T(8,128)(2,1)S(1)}, bf16[8,5120]{1,0:T(8,128)(2,1)}, u32[]{:S(2)}, u32[]{:S(2)}) collective-permute-start(bf16[8,5120]{1,0:T(8,128)(2,1)S(1)} %get-tuple-element.235), channel_id=1, source_target_pairs={{0,4},{1,3},{2,6},{3,1},{4,0},{5,7},{6,2},{7,5},{8,12},{9,11},{10,... | collective-permute-start | bytes 245768 | tf_op jit(solution)/shard_map/cond/branch_1_fun/ppermute | solution.py:342
  102.3 0.6 collective-permute-start.74
  103.0 1.2 collective-permute-done.72
  104.2 5.7 %collective-permute-start.76 = (bf16[8,5120]{1,0:T(8,128)(2,1)S(1)}, bf16[8,5120]{1,0:T(8,128)(2,1)}, u32[]{:S(2)}, u32[]{:S(2)}) collective-permute-start(bf16[8,5120]{1,0:T(8,128)(2,1)S(1)} %get-tuple-element.238), channel_id=1, source_target_pairs={{0,5},{1,2},{2,7},{3,0},{4,1},{5,6},{6,3},{7,4},{8,13},{9,10},{10,... | collective-permute-start | bytes 245768 | tf_op jit(solution)/shard_map/cond/branch_1_fun/ppermute | solution.py:342
  109.9 5.2 %collective-permute-done.70.refs_9_ = bf16[4,8,5120]{2,1,0:T(8,128)(2,1)S(1)} collective-permute-done((bf16[4,8,5120]{2,1,0:T(8,128)(2,1)S(1)}, bf16[4,8,5120]{2,1,0:T(8,128)(2,1)S(1)}, u32[]{:S(2)}, u32[]{:S(2)}) %collective-permute-start.70) | collective-permute-done | bytes 327712 | tf_op jit(solution)/shard_map/cond/branch_1_fun/ppermute | solution.py:317
  115.5 1.0 branch_1_fun.20
  116.5 4.0 %collective-permute-done.77 = bf16[8,5120]{1,0:T(8,128)(2,1)} collective-permute-done((bf16[8,5120]{1,0:T(8,128)(2,1)S(1)}, bf16[8,5120]{1,0:T(8,128)(2,1)}, u32[]{:S(2)}, u32[]{:S(2)}) %collective-permute-start.77) | collective-permute-done | bytes 81952 | tf_op jit(solution)/shard_map/cond/branch_1_fun/ppermute | solution.py:342
  120.7 1.0 collective-permute-start.164
  121.7 2.5 %collective-permute-start.166 = (bf16[8,5120]{1,0:T(8,128)(2,1)S(1)}, bf16[8,5120]{1,0:T(8,128)(2,1)S(1)}, u32[]{:S(2)}, u32[]{:S(2)}) collective-permute-start(bf16[8,5120]{1,0:T(8,128)(2,1)S(1)} %get-tuple-element.411), channel_id=1, source_target_pairs={{0,6},{1,7},{2,4},{3,5},{4,2},{5,3},{6,0},{7,1},{8,14},{9,15},{10,... | collective-permute-start | bytes 245768 | tf_op jit(solution)/shard_map/ppermute | solution.py:342
  124.3 1.6 %collective-permute-start.168 = (bf16[8,5120]{1,0:T(8,128)(2,1)S(1)}, bf16[8,5120]{1,0:T(8,128)(2,1)S(1)}, u32[]{:S(2)}, u32[]{:S(2)}) collective-permute-start(bf16[8,5120]{1,0:T(8,128)(2,1)S(1)} %get-tuple-element.413), channel_id=1, source_target_pairs={{0,5},{1,2},{2,7},{3,0},{4,1},{5,6},{6,3},{7,4},{8,13},{9,10},{10,... | collective-permute-start | bytes 245768 | tf_op jit(solution)/shard_map/ppermute | solution.py:342
  126.4 2.0 %shard_map.88 = bf16[8,8,5120]{2,1,0:T(8,128)(2,1)} custom-call(bf16[8,5120]{1,0:T(8,128)(2,1)S(1)} %get-tuple-element.415.refs_0_, bf16[8,5120]{1,0:T(8,128)(2,1)} %get-tuple-element.416.refs_1_, bf16[8,5120]{1,0:T(8,128)(2,1)} %get-tuple-element.417.refs_2_, bf16[8,5120]{1,0:T(8,128)(2,1)} %get-tuple-element.418.refs_3_, ...), custom_call_target="tpu_custom_call" | custom-call | tf_op jit(solution)/shard_map/pallas_call | solution.py:81
  129.6 1.9 %collective-permute-done.169.refs_7_ = bf16[8,5120]{1,0:T(8,128)(2,1)S(1)} collective-permute-done((bf16[8,5120]{1,0:T(8,128)(2,1)S(1)}, bf16[8,5120]{1,0:T(8,128)(2,1)S(1)}, u32[]{:S(2)}, u32[]{:S(2)}) %collective-permute-start.169) | collective-permute-done | bytes 81952 | tf_op jit(solution)/shard_map/ppermute | solution.py:342
  131.5 0.9 shard_map.87
  (69 shorter events, 6.3 us)
Async XLA Ops:
  0.6 1.1 copy-start
  1.8 5.8 %collective-permute-start.156 = (bf16[8,5120]{1,0:T(8,128)(2,1)S(1)}, bf16[8,5120]{1,0:T(8,128)(2,1)S(1)}, u32[]{:S(2)}, u32[]{:S(2)}) collective-permute-start(bf16[8,5120]{1,0:T(8,128)(2,1)S(1)} %get-tuple-element.399), channel_id=1, source_target_pairs={{0,1},{1,0},{2,3},{3,2},{4,5},{5,4},{6,7},{7,6},{8,9},{9,8},{10,11... | collective-permute-start | bytes 245768 | tf_op jit(solution)/shard_map/ppermute | solution.py:342
  2.3 5.9 %collective-permute-start.157 = (bf16[8,5120]{1,0:T(8,128)(2,1)S(1)}, bf16[8,5120]{1,0:T(8,128)(2,1)S(1)}, u32[]{:S(2)}, u32[]{:S(2)}) collective-permute-start(bf16[8,5120]{1,0:T(8,128)(2,1)S(1)} %get-tuple-element.400), channel_id=1, source_target_pairs={{0,2},{1,5},{2,0},{3,7},{4,6},{5,1},{6,4},{7,3},{8,10},{9,13},{10,... | collective-permute-start | bytes 245768 | tf_op jit(solution)/shard_map/ppermute | solution.py:342
  4.9 7.7 %collective-permute-start.158 = (bf16[8,5120]{1,0:T(8,128)(2,1)S(1)}, bf16[8,5120]{1,0:T(8,128)(2,1)S(1)}, u32[]{:S(2)}, u32[]{:S(2)}) collective-permute-start(bf16[8,5120]{1,0:T(8,128)(2,1)S(1)} %get-tuple-element.401), channel_id=1, source_target_pairs={{0,4},{1,3},{2,6},{3,1},{4,0},{5,7},{6,2},{7,5},{8,12},{9,11},{10,... | collective-permute-start | bytes 245768 | tf_op jit(solution)/shard_map/ppermute | solution.py:342
  6.5 6.2 %collective-permute-start.159 = (bf16[8,5120]{1,0:T(8,128)(2,1)S(1)}, bf16[8,5120]{1,0:T(8,128)(2,1)S(1)}, u32[]{:S(2)}, u32[]{:S(2)}) collective-permute-start(bf16[8,5120]{1,0:T(8,128)(2,1)S(1)} %get-tuple-element.402), channel_id=1, source_target_pairs={{0,6},{1,7},{2,4},{3,5},{4,2},{5,3},{6,0},{7,1},{8,14},{9,15},{10,... | collective-permute-start | bytes 245768 | tf_op jit(solution)/shard_map/ppermute | solution.py:342
  6.5 6.2 %collective-permute-start.160 = (bf16[8,5120]{1,0:T(8,128)(2,1)S(1)}, bf16[8,5120]{1,0:T(8,128)(2,1)S(1)}, u32[]{:S(2)}, u32[]{:S(2)}) collective-permute-start(bf16[8,5120]{1,0:T(8,128)(2,1)S(1)} %get-tuple-element.403), channel_id=1, source_target_pairs={{0,3},{1,4},{2,1},{3,6},{4,7},{5,0},{6,5},{7,2},{8,11},{9,12},{10,... | collective-permute-start | bytes 245768 | tf_op jit(solution)/shard_map/ppermute | solution.py:342
  7.6 6.6 %collective-permute-start.161 = (bf16[8,5120]{1,0:T(8,128)(2,1)S(1)}, bf16[8,5120]{1,0:T(8,128)(2,1)S(1)}, u32[]{:S(2)}, u32[]{:S(2)}) collective-permute-start(bf16[8,5120]{1,0:T(8,128)(2,1)S(1)} %get-tuple-element.404), channel_id=1, source_target_pairs={{0,5},{1,2},{2,7},{3,0},{4,1},{5,6},{6,3},{7,4},{8,13},{9,10},{10,... | collective-permute-start | bytes 245768 | tf_op jit(solution)/shard_map/ppermute | solution.py:342
  8.2 6.0 %collective-permute-start.162 = (bf16[8,5120]{1,0:T(8,128)(2,1)S(1)}, bf16[8,5120]{1,0:T(8,128)(2,1)S(1)}, u32[]{:S(2)}, u32[]{:S(2)}) collective-permute-start(bf16[8,5120]{1,0:T(8,128)(2,1)S(1)} %get-tuple-element.405), channel_id=1, source_target_pairs={{0,7},{1,6},{2,5},{3,4},{4,3},{5,2},{6,1},{7,0},{8,15},{9,14},{10,... | collective-permute-start | bytes 245768 | tf_op jit(solution)/shard_map/ppermute | solution.py:342
  14.2 3.3 %copy-start.10 = (bf16[8,8,5120]{2,1,0:T(8,128)(2,1)S(1)}, bf16[8,8,5120]{2,1,0:T(8,128)(2,1)}, u32[]{:S(2)}) copy-start(bf16[8,8,5120]{2,1,0:T(8,128)(2,1)} %get-tuple-element.178.refs_0_) | copy-start | bytes 1966084 | tf_op jit(solution)/shard_map/conditional
  14.9 20.6 %collective-permute-start.46 = (bf16[4,8,5120]{2,1,0:T(8,128)(2,1)S(1)}, bf16[4,8,5120]{2,1,0:T(8,128)(2,1)S(1)}, u32[]{:S(2)}, u32[]{:S(2)}) collective-permute-start(bf16[4,8,5120]{2,1,0:T(8,128)(2,1)S(1)} %branch_1_fun.11.refs_1_), channel_id=1, source_target_pairs={{0,8},{1,9},{2,10},{3,11},{4,12},{5,13},{6,14},{7,15},{8,0},{9,1},... | collective-permute-start | bytes 983048 | tf_op jit(solution)/shard_map/cond/branch_1_fun/ppermute | solution.py:317
  17.6 4.1 %collective-permute-start.39 = (bf16[8,5120]{1,0:T(8,128)(2,1)S(1)}, bf16[8,5120]{1,0:T(8,128)(2,1)S(1)}, u32[]{:S(2)}, u32[]{:S(2)}) collective-permute-start(bf16[8,5120]{1,0:T(8,128)(2,1)S(1)} %get-tuple-element.188), channel_id=1, source_target_pairs={{0,1},{1,0},{2,3},{3,2},{4,5},{5,4},{6,7},{7,6},{8,9},{9,8},{10,11... | collective-permute-start | bytes 245768 | tf_op jit(solution)/shard_map/cond/branch_1_fun/ppermute | solution.py:342
  18.2 5.1 %collective-permute-start.40 = (bf16[8,5120]{1,0:T(8,128)(2,1)S(1)}, bf16[8,5120]{1,0:T(8,128)(2,1)S(1)}, u32[]{:S(2)}, u32[]{:S(2)}) collective-permute-start(bf16[8,5120]{1,0:T(8,128)(2,1)S(1)} %get-tuple-element.189), channel_id=1, source_target_pairs={{0,2},{1,5},{2,0},{3,7},{4,6},{5,1},{6,4},{7,3},{8,10},{9,13},{10,... | collective-permute-start | bytes 245768 | tf_op jit(solution)/shard_map/cond/branch_1_fun/ppermute | solution.py:342
  19.4 9.9 %collective-permute-start.41 = (bf16[8,5120]{1,0:T(8,128)(2,1)S(1)}, bf16[8,5120]{1,0:T(8,128)(2,1)S(1)}, u32[]{:S(2)}, u32[]{:S(2)}) collective-permute-start(bf16[8,5120]{1,0:T(8,128)(2,1)S(1)} %get-tuple-element.190), channel_id=1, source_target_pairs={{0,4},{1,3},{2,6},{3,1},{4,0},{5,7},{6,2},{7,5},{8,12},{9,11},{10,... | collective-permute-start | bytes 245768 | tf_op jit(solution)/shard_map/cond/branch_1_fun/ppermute | solution.py:342
  20.6 8.7 %collective-permute-start.42 = (bf16[8,5120]{1,0:T(8,128)(2,1)S(1)}, bf16[8,5120]{1,0:T(8,128)(2,1)S(1)}, u32[]{:S(2)}, u32[]{:S(2)}) collective-permute-start(bf16[8,5120]{1,0:T(8,128)(2,1)S(1)} %get-tuple-element.191), channel_id=1, source_target_pairs={{0,6},{1,7},{2,4},{3,5},{4,2},{5,3},{6,0},{7,1},{8,14},{9,15},{10,... | collective-permute-start | bytes 245768 | tf_op jit(solution)/shard_map/cond/branch_1_fun/ppermute | solution.py:342
  21.7 7.6 %collective-permute-start.43 = (bf16[8,5120]{1,0:T(8,128)(2,1)S(1)}, bf16[8,5120]{1,0:T(8,128)(2,1)S(1)}, u32[]{:S(2)}, u32[]{:S(2)}) collective-permute-start(bf16[8,5120]{1,0:T(8,128)(2,1)S(1)} %get-tuple-element.192), channel_id=1, source_target_pairs={{0,3},{1,4},{2,1},{3,6},{4,7},{5,0},{6,5},{7,2},{8,11},{9,12},{10,... | collective-permute-start | bytes 245768 | tf_op jit(solution)/shard_map/cond/branch_1_fun/ppermute | solution.py:342
  23.2 8.1 %collective-permute-start.44 = (bf16[8,5120]{1,0:T(8,128)(2,1)S(1)}, bf16[8,5120]{1,0:T(8,128)(2,1)S(1)}, u32[]{:S(2)}, u32[]{:S(2)}) collective-permute-start(bf16[8,5120]{1,0:T(8,128)(2,1)S(1)} %get-tuple-element.193), channel_id=1, source_target_pairs={{0,5},{1,2},{2,7},{3,0},{4,1},{5,6},{6,3},{7,4},{8,13},{9,10},{10,... | collective-permute-start | bytes 245768 | tf_op jit(solution)/shard_map/cond/branch_1_fun/ppermute | solution.py:342
  29.3 6.2 %collective-permute-start.45 = (bf16[8,5120]{1,0:T(8,128)(2,1)S(1)}, bf16[8,5120]{1,0:T(8,128)(2,1)S(1)}, u32[]{:S(2)}, u32[]{:S(2)}) collective-permute-start(bf16[8,5120]{1,0:T(8,128)(2,1)S(1)} %get-tuple-element.194), channel_id=1, source_target_pairs={{0,7},{1,6},{2,5},{3,4},{4,3},{5,2},{6,1},{7,0},{8,15},{9,14},{10,... | collective-permute-start | bytes 245768 | tf_op jit(solution)/shard_map/cond/branch_1_fun/ppermute | solution.py:342
  35.5 21.3 %copy-start.2 = (bf16[128,5120]{1,0:T(8,128)(2,1)S(1)}, bf16[128,5120]{1,0:T(8,128)(2,1)}, u32[]{:S(2)}) copy-start(bf16[128,5120]{1,0:T(8,128)(2,1)} %get-tuple-element.203.refs_8_.refs_9_) | copy-start | bytes 3932164 | tf_op jit(solution)/shard_map/conditional
  35.5 21.3 %copy-start.6 = (bf16[128,5120]{1,0:T(8,128)(2,1)S(1)}, bf16[128,5120]{1,0:T(8,128)(2,1)}, u32[]{:S(2)}) copy-start(bf16[128,5120]{1,0:T(8,128)(2,1)} %get-tuple-element.204.refs_9_.refs_8_) | copy-start | bytes 3932164 | tf_op jit(solution)/shard_map/conditional
  36.2 21.8 %collective-permute-start.47 = (bf16[4,8,5120]{2,1,0:T(8,128)(2,1)S(1)}, bf16[4,8,5120]{2,1,0:T(8,128)(2,1)S(1)}, u32[]{:S(2)}, u32[]{:S(2)}) collective-permute-start(bf16[4,8,5120]{2,1,0:T(8,128)(2,1)S(1)} %branch_1_fun.13.refs_10_), channel_id=1, source_target_pairs={{0,8},{1,9},{2,10},{3,11},{4,12},{5,13},{6,14},{7,15},{8,0},{9,1},... | collective-permute-start | bytes 983048 | tf_op jit(solution)/shard_map/cond/branch_1_fun/ppermute | solution.py:317
  38.4 3.6 %collective-permute-start.48 = (bf16[8,5120]{1,0:T(8,128)(2,1)S(1)}, bf16[8,5120]{1,0:T(8,128)(2,1)S(1)}, u32[]{:S(2)}, u32[]{:S(2)}) collective-permute-start(bf16[8,5120]{1,0:T(8,128)(2,1)S(1)} %get-tuple-element.196), channel_id=1, source_target_pairs={{0,1},{1,0},{2,3},{3,2},{4,5},{5,4},{6,7},{7,6},{8,9},{9,8},{10,11... | collective-permute-start | bytes 245768 | tf_op jit(solution)/shard_map/cond/branch_1_fun/ppermute | solution.py:342
  38.5 4.5 %collective-permute-start.49 = (bf16[8,5120]{1,0:T(8,128)(2,1)S(1)}, bf16[8,5120]{1,0:T(8,128)(2,1)S(1)}, u32[]{:S(2)}, u32[]{:S(2)}) collective-permute-start(bf16[8,5120]{1,0:T(8,128)(2,1)S(1)} %get-tuple-element.197), channel_id=1, source_target_pairs={{0,2},{1,5},{2,0},{3,7},{4,6},{5,1},{6,4},{7,3},{8,10},{9,13},{10,... | collective-permute-start | bytes 245768 | tf_op jit(solution)/shard_map/cond/branch_1_fun/ppermute | solution.py:342
  38.8 8.9 %collective-permute-start.50 = (bf16[8,5120]{1,0:T(8,128)(2,1)S(1)}, bf16[8,5120]{1,0:T(8,128)(2,1)S(1)}, u32[]{:S(2)}, u32[]{:S(2)}) collective-permute-start(bf16[8,5120]{1,0:T(8,128)(2,1)S(1)} %get-tuple-element.198), channel_id=1, source_target_pairs={{0,4},{1,3},{2,6},{3,1},{4,0},{5,7},{6,2},{7,5},{8,12},{9,11},{10,... | collective-permute-start | bytes 245768 | tf_op jit(solution)/shard_map/cond/branch_1_fun/ppermute | solution.py:342
  42.0 6.8 %collective-permute-start.51 = (bf16[8,5120]{1,0:T(8,128)(2,1)S(1)}, bf16[8,5120]{1,0:T(8,128)(2,1)S(1)}, u32[]{:S(2)}, u32[]{:S(2)}) collective-permute-start(bf16[8,5120]{1,0:T(8,128)(2,1)S(1)} %get-tuple-element.199), channel_id=1, source_target_pairs={{0,6},{1,7},{2,4},{3,5},{4,2},{5,3},{6,0},{7,1},{8,14},{9,15},{10,... | collective-permute-start | bytes 245768 | tf_op jit(solution)/shard_map/cond/branch_1_fun/ppermute | solution.py:342
  42.1 11.9 %collective-permute-start.52 = (bf16[8,5120]{1,0:T(8,128)(2,1)S(1)}, bf16[8,5120]{1,0:T(8,128)(2,1)S(1)}, u32[]{:S(2)}, u32[]{:S(2)}) collective-permute-start(bf16[8,5120]{1,0:T(8,128)(2,1)S(1)} %get-tuple-element.200), channel_id=1, source_target_pairs={{0,3},{1,4},{2,1},{3,6},{4,7},{5,0},{6,5},{7,2},{8,11},{9,12},{10,... | collective-permute-start | bytes 245768 | tf_op jit(solution)/shard_map/cond/branch_1_fun/ppermute | solution.py:342
  43.1 10.9 %collective-permute-start.53 = (bf16[8,5120]{1,0:T(8,128)(2,1)S(1)}, bf16[8,5120]{1,0:T(8,128)(2,1)S(1)}, u32[]{:S(2)}, u32[]{:S(2)}) collective-permute-start(bf16[8,5120]{1,0:T(8,128)(2,1)S(1)} %get-tuple-element.201), channel_id=1, source_target_pairs={{0,5},{1,2},{2,7},{3,0},{4,1},{5,6},{6,3},{7,4},{8,13},{9,10},{10,... | collective-permute-start | bytes 245768 | tf_op jit(solution)/shard_map/cond/branch_1_fun/ppermute | solution.py:342
  47.7 9.1 %collective-permute-start.54 = (bf16[8,5120]{1,0:T(8,128)(2,1)S(1)}, bf16[8,5120]{1,0:T(8,128)(2,1)S(1)}, u32[]{:S(2)}, u32[]{:S(2)}) collective-permute-start(bf16[8,5120]{1,0:T(8,128)(2,1)S(1)} %get-tuple-element.202), channel_id=1, source_target_pairs={{0,7},{1,6},{2,5},{3,4},{4,3},{5,2},{6,1},{7,0},{8,15},{9,14},{10,... | collective-permute-start | bytes 245768 | tf_op jit(solution)/shard_map/cond/branch_1_fun/ppermute | solution.py:342
  58.8 4.2 %collective-permute-start.55 = (bf16[2,8,5120]{2,1,0:T(8,128)(2,1)S(1)}, bf16[2,8,5120]{2,1,0:T(8,128)(2,1)S(1)}, u32[]{:S(2)}, u32[]{:S(2)}) collective-permute-start(bf16[2,8,5120]{2,1,0:T(8,128)(2,1)S(1)} %get-tuple-element.207), channel_id=1, source_target_pairs={{0,1},{1,0},{2,3},{3,2},{4,5},{5,4},{6,7},{7,6},{8,9},{9,8},{10,11... | collective-permute-start | bytes 491528 | tf_op jit(solution)/shard_map/cond/branch_1_fun/ppermute | solution.py:342
  59.4 9.0 %collective-permute-start.56 = (bf16[2,8,5120]{2,1,0:T(8,128)(2,1)S(1)}, bf16[2,8,5120]{2,1,0:T(8,128)(2,1)S(1)}, u32[]{:S(2)}, u32[]{:S(2)}) collective-permute-start(bf16[2,8,5120]{2,1,0:T(8,128)(2,1)S(1)} %get-tuple-element.208), channel_id=1, source_target_pairs={{0,2},{1,5},{2,0},{3,7},{4,6},{5,1},{6,4},{7,3},{8,10},{9,13},{10,... | collective-permute-start | bytes 491528 | tf_op jit(solution)/shard_map/cond/branch_1_fun/ppermute | solution.py:342
  59.9 8.5 %collective-permute-start.57 = (bf16[2,8,5120]{2,1,0:T(8,128)(2,1)S(1)}, bf16[2,8,5120]{2,1,0:T(8,128)(2,1)S(1)}, u32[]{:S(2)}, u32[]{:S(2)}) collective-permute-start(bf16[2,8,5120]{2,1,0:T(8,128)(2,1)S(1)} %get-tuple-element.209), channel_id=1, source_target_pairs={{0,4},{1,3},{2,6},{3,1},{4,0},{5,7},{6,2},{7,5},{8,12},{9,11},{10,... | collective-permute-start | bytes 491528 | tf_op jit(solution)/shard_map/cond/branch_1_fun/ppermute | solution.py:342
  59.9 11.0 %collective-permute-start.58 = (bf16[2,8,5120]{2,1,0:T(8,128)(2,1)S(1)}, bf16[2,8,5120]{2,1,0:T(8,128)(2,1)S(1)}, u32[]{:S(2)}, u32[]{:S(2)}) collective-permute-start(bf16[2,8,5120]{2,1,0:T(8,128)(2,1)S(1)} %get-tuple-element.210), channel_id=1, source_target_pairs={{0,6},{1,7},{2,4},{3,5},{4,2},{5,3},{6,0},{7,1},{8,14},{9,15},{10,... | collective-permute-start | bytes 491528 | tf_op jit(solution)/shard_map/cond/branch_1_fun/ppermute | solution.py:342
  62.9 8.3 %collective-permute-start.59 = (bf16[2,8,5120]{2,1,0:T(8,128)(2,1)S(1)}, bf16[2,8,5120]{2,1,0:T(8,128)(2,1)S(1)}, u32[]{:S(2)}, u32[]{:S(2)}) collective-permute-start(bf16[2,8,5120]{2,1,0:T(8,128)(2,1)S(1)} %get-tuple-element.211), channel_id=1, source_target_pairs={{0,3},{1,4},{2,1},{3,6},{4,7},{5,0},{6,5},{7,2},{8,11},{9,12},{10,... | collective-permute-start | bytes 491528 | tf_op jit(solution)/shard_map/cond/branch_1_fun/ppermute | solution.py:342
  62.9 9.0 %collective-permute-start.60 = (bf16[2,8,5120]{2,1,0:T(8,128)(2,1)S(1)}, bf16[2,8,5120]{2,1,0:T(8,128)(2,1)S(1)}, u32[]{:S(2)}, u32[]{:S(2)}) collective-permute-start(bf16[2,8,5120]{2,1,0:T(8,128)(2,1)S(1)} %get-tuple-element.212), channel_id=1, source_target_pairs={{0,5},{1,2},{2,7},{3,0},{4,1},{5,6},{6,3},{7,4},{8,13},{9,10},{10,... | collective-permute-start | bytes 491528 | tf_op jit(solution)/shard_map/cond/branch_1_fun/ppermute | solution.py:342
  68.4 7.6 %collective-permute-start.61 = (bf16[2,8,5120]{2,1,0:T(8,128)(2,1)S(1)}, bf16[2,8,5120]{2,1,0:T(8,128)(2,1)S(1)}, u32[]{:S(2)}, u32[]{:S(2)}) collective-permute-start(bf16[2,8,5120]{2,1,0:T(8,128)(2,1)S(1)} %get-tuple-element.213), channel_id=1, source_target_pairs={{0,7},{1,6},{2,5},{3,4},{4,3},{5,2},{6,1},{7,0},{8,15},{9,14},{10,... | collective-permute-start | bytes 491528 | tf_op jit(solution)/shard_map/cond/branch_1_fun/ppermute | solution.py:342
  76.9 20.0 %collective-permute-start.69 = (bf16[4,8,5120]{2,1,0:T(8,128)(2,1)S(1)}, bf16[4,8,5120]{2,1,0:T(8,128)(2,1)S(1)}, u32[]{:S(2)}, u32[]{:S(2)}) collective-permute-start(bf16[4,8,5120]{2,1,0:T(8,128)(2,1)S(1)} %branch_1_fun.17.refs_10_), channel_id=1, source_target_pairs={{0,8},{1,9},{2,10},{3,11},{4,12},{5,13},{6,14},{7,15},{8,0},{9,1},... | collective-permute-start | bytes 983048 | tf_op jit(solution)/shard_map/cond/branch_1_fun/ppermute | solution.py:317
  78.2 3.8 %collective-permute-start.62 = (bf16[8,5120]{1,0:T(8,128)(2,1)S(1)}, bf16[8,5120]{1,0:T(8,128)(2,1)S(1)}, u32[]{:S(2)}, u32[]{:S(2)}) collective-permute-start(bf16[8,5120]{1,0:T(8,128)(2,1)S(1)} %get-tuple-element.217), channel_id=1, source_target_pairs={{0,1},{1,0},{2,3},{3,2},{4,5},{5,4},{6,7},{7,6},{8,9},{9,8},{10,11... | collective-permute-start | bytes 245768 | tf_op jit(solution)/shard_map/cond/branch_1_fun/ppermute | solution.py:342
  78.5 4.9 %collective-permute-start.63 = (bf16[8,5120]{1,0:T(8,128)(2,1)S(1)}, bf16[8,5120]{1,0:T(8,128)(2,1)S(1)}, u32[]{:S(2)}, u32[]{:S(2)}) collective-permute-start(bf16[8,5120]{1,0:T(8,128)(2,1)S(1)} %get-tuple-element.218), channel_id=1, source_target_pairs={{0,2},{1,5},{2,0},{3,7},{4,6},{5,1},{6,4},{7,3},{8,10},{9,13},{10,... | collective-permute-start | bytes 245768 | tf_op jit(solution)/shard_map/cond/branch_1_fun/ppermute | solution.py:342
  79.7 8.6 %collective-permute-start.64 = (bf16[8,5120]{1,0:T(8,128)(2,1)S(1)}, bf16[8,5120]{1,0:T(8,128)(2,1)S(1)}, u32[]{:S(2)}, u32[]{:S(2)}) collective-permute-start(bf16[8,5120]{1,0:T(8,128)(2,1)S(1)} %get-tuple-element.219), channel_id=1, source_target_pairs={{0,4},{1,3},{2,6},{3,1},{4,0},{5,7},{6,2},{7,5},{8,12},{9,11},{10,... | collective-permute-start | bytes 245768 | tf_op jit(solution)/shard_map/cond/branch_1_fun/ppermute | solution.py:342
  81.2 8.1 %collective-permute-start.65 = (bf16[8,5120]{1,0:T(8,128)(2,1)S(1)}, bf16[8,5120]{1,0:T(8,128)(2,1)S(1)}, u32[]{:S(2)}, u32[]{:S(2)}) collective-permute-start(bf16[8,5120]{1,0:T(8,128)(2,1)S(1)} %get-tuple-element.220), channel_id=1, source_target_pairs={{0,6},{1,7},{2,4},{3,5},{4,2},{5,3},{6,0},{7,1},{8,14},{9,15},{10,... | collective-permute-start | bytes 245768 | tf_op jit(solution)/shard_map/cond/branch_1_fun/ppermute | solution.py:342
  82.0 7.2 %collective-permute-start.66 = (bf16[8,5120]{1,0:T(8,128)(2,1)S(1)}, bf16[8,5120]{1,0:T(8,128)(2,1)S(1)}, u32[]{:S(2)}, u32[]{:S(2)}) collective-permute-start(bf16[8,5120]{1,0:T(8,128)(2,1)S(1)} %get-tuple-element.221), channel_id=1, source_target_pairs={{0,3},{1,4},{2,1},{3,6},{4,7},{5,0},{6,5},{7,2},{8,11},{9,12},{10,... | collective-permute-start | bytes 245768 | tf_op jit(solution)/shard_map/cond/branch_1_fun/ppermute | solution.py:342
  83.3 7.1 %collective-permute-start.67 = (bf16[8,5120]{1,0:T(8,128)(2,1)S(1)}, bf16[8,5120]{1,0:T(8,128)(2,1)S(1)}, u32[]{:S(2)}, u32[]{:S(2)}) collective-permute-start(bf16[8,5120]{1,0:T(8,128)(2,1)S(1)} %get-tuple-element.222), channel_id=1, source_target_pairs={{0,5},{1,2},{2,7},{3,0},{4,1},{5,6},{6,3},{7,4},{8,13},{9,10},{10,... | collective-permute-start | bytes 245768 | tf_op jit(solution)/shard_map/cond/branch_1_fun/ppermute | solution.py:342
  88.2 8.7 %collective-permute-start.68 = (bf16[8,5120]{1,0:T(8,128)(2,1)S(1)}, bf16[8,5120]{1,0:T(8,128)(2,1)S(1)}, u32[]{:S(2)}, u32[]{:S(2)}) collective-permute-start(bf16[8,5120]{1,0:T(8,128)(2,1)S(1)} %get-tuple-element.223), channel_id=1, source_target_pairs={{0,7},{1,6},{2,5},{3,4},{4,3},{5,2},{6,1},{7,0},{8,15},{9,14},{10,... | collective-permute-start | bytes 245768 | tf_op jit(solution)/shard_map/cond/branch_1_fun/ppermute | solution.py:342
  97.7 17.3 %collective-permute-start.70 = (bf16[4,8,5120]{2,1,0:T(8,128)(2,1)S(1)}, bf16[4,8,5120]{2,1,0:T(8,128)(2,1)S(1)}, u32[]{:S(2)}, u32[]{:S(2)}) collective-permute-start(bf16[4,8,5120]{2,1,0:T(8,128)(2,1)S(1)} %branch_1_fun.19.refs_10_), channel_id=1, source_target_pairs={{0,8},{1,9},{2,10},{3,11},{4,12},{5,13},{6,14},{7,15},{8,0},{9,1},... | collective-permute-start | bytes 983048 | tf_op jit(solution)/shard_map/cond/branch_1_fun/ppermute | solution.py:317
  98.8 4.2 %collective-permute-start.71 = (bf16[8,5120]{1,0:T(8,128)(2,1)S(1)}, bf16[8,5120]{1,0:T(8,128)(2,1)}, u32[]{:S(2)}, u32[]{:S(2)}) collective-permute-start(bf16[8,5120]{1,0:T(8,128)(2,1)S(1)} %get-tuple-element.233), channel_id=1, source_target_pairs={{0,1},{1,0},{2,3},{3,2},{4,5},{5,4},{6,7},{7,6},{8,9},{9,8},{10,11... | collective-permute-start | bytes 245768 | tf_op jit(solution)/shard_map/cond/branch_1_fun/ppermute | solution.py:342
  99.5 4.7 %collective-permute-start.72 = (bf16[8,5120]{1,0:T(8,128)(2,1)S(1)}, bf16[8,5120]{1,0:T(8,128)(2,1)}, u32[]{:S(2)}, u32[]{:S(2)}) collective-permute-start(bf16[8,5120]{1,0:T(8,128)(2,1)S(1)} %get-tuple-element.234), channel_id=1, source_target_pairs={{0,2},{1,5},{2,0},{3,7},{4,6},{5,1},{6,4},{7,3},{8,10},{9,13},{10,... | collective-permute-start | bytes 245768 | tf_op jit(solution)/shard_map/cond/branch_1_fun/ppermute | solution.py:342
  100.4 16.2 %collective-permute-start.73 = (bf16[8,5120]{1,0:T(8,128)(2,1)S(1)}, bf16[8,5120]{1,0:T(8,128)(2,1)}, u32[]{:S(2)}, u32[]{:S(2)}) collective-permute-start(bf16[8,5120]{1,0:T(8,128)(2,1)S(1)} %get-tuple-element.235), channel_id=1, source_target_pairs={{0,4},{1,3},{2,6},{3,1},{4,0},{5,7},{6,2},{7,5},{8,12},{9,11},{10,... | collective-permute-start | bytes 245768 | tf_op jit(solution)/shard_map/cond/branch_1_fun/ppermute | solution.py:342
  102.3 14.2 %collective-permute-start.74 = (bf16[8,5120]{1,0:T(8,128)(2,1)S(1)}, bf16[8,5120]{1,0:T(8,128)(2,1)}, u32[]{:S(2)}, u32[]{:S(2)}) collective-permute-start(bf16[8,5120]{1,0:T(8,128)(2,1)S(1)} %get-tuple-element.236), channel_id=1, source_target_pairs={{0,6},{1,7},{2,4},{3,5},{4,2},{5,3},{6,0},{7,1},{8,14},{9,15},{10,... | collective-permute-start | bytes 245768 | tf_op jit(solution)/shard_map/cond/branch_1_fun/ppermute | solution.py:342
  103.0 13.6 %collective-permute-start.75 = (bf16[8,5120]{1,0:T(8,128)(2,1)S(1)}, bf16[8,5120]{1,0:T(8,128)(2,1)}, u32[]{:S(2)}, u32[]{:S(2)}) collective-permute-start(bf16[8,5120]{1,0:T(8,128)(2,1)S(1)} %get-tuple-element.237), channel_id=1, source_target_pairs={{0,3},{1,4},{2,1},{3,6},{4,7},{5,0},{6,5},{7,2},{8,11},{9,12},{10,... | collective-permute-start | bytes 245768 | tf_op jit(solution)/shard_map/cond/branch_1_fun/ppermute | solution.py:342
  104.2 12.4 %collective-permute-start.76 = (bf16[8,5120]{1,0:T(8,128)(2,1)S(1)}, bf16[8,5120]{1,0:T(8,128)(2,1)}, u32[]{:S(2)}, u32[]{:S(2)}) collective-permute-start(bf16[8,5120]{1,0:T(8,128)(2,1)S(1)} %get-tuple-element.238), channel_id=1, source_target_pairs={{0,5},{1,2},{2,7},{3,0},{4,1},{5,6},{6,3},{7,4},{8,13},{9,10},{10,... | collective-permute-start | bytes 245768 | tf_op jit(solution)/shard_map/cond/branch_1_fun/ppermute | solution.py:342
  115.1 5.5 %collective-permute-start.77 = (bf16[8,5120]{1,0:T(8,128)(2,1)S(1)}, bf16[8,5120]{1,0:T(8,128)(2,1)}, u32[]{:S(2)}, u32[]{:S(2)}) collective-permute-start(bf16[8,5120]{1,0:T(8,128)(2,1)S(1)} %get-tuple-element.239), channel_id=1, source_target_pairs={{0,7},{1,6},{2,5},{3,4},{4,3},{5,2},{6,1},{7,0},{8,15},{9,14},{10,... | collective-permute-start | bytes 245768 | tf_op jit(solution)/shard_map/cond/branch_1_fun/ppermute | solution.py:342
  120.6 11.8 %copy-start.13 = (bf16[128,5120]{1,0:T(8,128)(2,1)}, bf16[128,5120]{1,0:T(8,128)(2,1)S(1)}, u32[]{:S(2)}) copy-start(bf16[128,5120]{1,0:T(8,128)(2,1)S(1)} %get-tuple-element.406) | copy-start | bytes 3932164
  120.6 3.7 %collective-permute-start.163 = (bf16[8,5120]{1,0:T(8,128)(2,1)S(1)}, bf16[8,5120]{1,0:T(8,128)(2,1)S(1)}, u32[]{:S(2)}, u32[]{:S(2)}) collective-permute-start(bf16[8,5120]{1,0:T(8,128)(2,1)S(1)} %get-tuple-element.408), channel_id=1, source_target_pairs={{0,1},{1,0},{2,3},{3,2},{4,5},{5,4},{6,7},{7,6},{8,9},{9,8},{10,11... | collective-permute-start | bytes 245768 | tf_op jit(solution)/shard_map/ppermute | solution.py:342
  120.7 5.3 %collective-permute-start.164 = (bf16[8,5120]{1,0:T(8,128)(2,1)S(1)}, bf16[8,5120]{1,0:T(8,128)(2,1)S(1)}, u32[]{:S(2)}, u32[]{:S(2)}) collective-permute-start(bf16[8,5120]{1,0:T(8,128)(2,1)S(1)} %get-tuple-element.409), channel_id=1, source_target_pairs={{0,2},{1,5},{2,0},{3,7},{4,6},{5,1},{6,4},{7,3},{8,10},{9,13},{10,... | collective-permute-start | bytes 245768 | tf_op jit(solution)/shard_map/ppermute | solution.py:342
  121.7 6.8 %collective-permute-start.165 = (bf16[8,5120]{1,0:T(8,128)(2,1)S(1)}, bf16[8,5120]{1,0:T(8,128)(2,1)S(1)}, u32[]{:S(2)}, u32[]{:S(2)}) collective-permute-start(bf16[8,5120]{1,0:T(8,128)(2,1)S(1)} %get-tuple-element.410), channel_id=1, source_target_pairs={{0,4},{1,3},{2,6},{3,1},{4,0},{5,7},{6,2},{7,5},{8,12},{9,11},{10,... | collective-permute-start | bytes 245768 | tf_op jit(solution)/shard_map/ppermute | solution.py:342
  121.7 6.8 %collective-permute-start.166 = (bf16[8,5120]{1,0:T(8,128)(2,1)S(1)}, bf16[8,5120]{1,0:T(8,128)(2,1)S(1)}, u32[]{:S(2)}, u32[]{:S(2)}) collective-permute-start(bf16[8,5120]{1,0:T(8,128)(2,1)S(1)} %get-tuple-element.411), channel_id=1, source_target_pairs={{0,6},{1,7},{2,4},{3,5},{4,2},{5,3},{6,0},{7,1},{8,14},{9,15},{10,... | collective-permute-start | bytes 245768 | tf_op jit(solution)/shard_map/ppermute | solution.py:342
  124.2 4.8 %collective-permute-start.167 = (bf16[8,5120]{1,0:T(8,128)(2,1)S(1)}, bf16[8,5120]{1,0:T(8,128)(2,1)S(1)}, u32[]{:S(2)}, u32[]{:S(2)}) collective-permute-start(bf16[8,5120]{1,0:T(8,128)(2,1)S(1)} %get-tuple-element.412), channel_id=1, source_target_pairs={{0,3},{1,4},{2,1},{3,6},{4,7},{5,0},{6,5},{7,2},{8,11},{9,12},{10,... | collective-permute-start | bytes 245768 | tf_op jit(solution)/shard_map/ppermute | solution.py:342
  124.3 5.2 %collective-permute-start.168 = (bf16[8,5120]{1,0:T(8,128)(2,1)S(1)}, bf16[8,5120]{1,0:T(8,128)(2,1)S(1)}, u32[]{:S(2)}, u32[]{:S(2)}) collective-permute-start(bf16[8,5120]{1,0:T(8,128)(2,1)S(1)} %get-tuple-element.413), channel_id=1, source_target_pairs={{0,5},{1,2},{2,7},{3,0},{4,1},{5,6},{6,3},{7,4},{8,13},{9,10},{10,... | collective-permute-start | bytes 245768 | tf_op jit(solution)/shard_map/ppermute | solution.py:342
  126.0 5.5 %collective-permute-start.169 = (bf16[8,5120]{1,0:T(8,128)(2,1)S(1)}, bf16[8,5120]{1,0:T(8,128)(2,1)S(1)}, u32[]{:S(2)}, u32[]{:S(2)}) collective-permute-start(bf16[8,5120]{1,0:T(8,128)(2,1)S(1)} %get-tuple-element.414), channel_id=1, source_target_pairs={{0,7},{1,6},{2,5},{3,4},{4,3},{5,2},{6,1},{7,0},{8,15},{9,14},{10,... | collective-permute-start | bytes 245768 | tf_op jit(solution)/shard_map/ppermute | solution.py:342
where the time goes:
time: 133 us; the launch traced here: 132 us
  starting transfers between devices  63.7 us (48%)
  waiting for transfers between devices  52.1 us (39%)
  Pallas kernels  13.4 us (10%)
  between operations  1.33 us (1%)
    ppermute x49, starting transfers between devices, exchange(): lax.ppermute(piece, 'dp', [(i, i ^ step[i % 2]) for i in range(devices)])  59.4 us
    ppermute x49, waiting for transfers between devices, exchange(): lax.ppermute(piece, 'dp', [(i, i ^ step[i % 2]) for i in range(devices)])  46.9 us
    pallas_call x14, Pallas kernels, call(): pl.pallas_call(lambda *refs: kernel(*refs[:given], *refs[given + len(afte...  11.9 us
    ppermute x4, waiting for transfers between devices, across(): return lax.ppermute(array, 'dp', pairs)  5.2 us
    ppermute x4, starting transfers between devices, across(): return lax.ppermute(array, 'dp', pairs)  4.33 us
  transfers between devices with their start and end apart: 53, of which 24 were waited for; matrix products, arithmetic and copies ran while one was open for 0% of the time, Pallas kernels for 7%

commit v1 on v0

--- a/solution.py
+++ b/solution.py
@@ -57,7 +57,7 @@
     return grad_rows, grads[:1], grads[1:]
 
 
-STEPS = ((0, 0), (1, 1), (2, 4), (4, 2), (6, 6), (3, 5), (5, 3), (7, 7))
+STEPS = ((0, 0), (2, 4), (4, 2), (6, 6), (3, 5), (5, 3), (7, 7), (1, 1))
 
 
 def partners(sending):

time: 133 us -> 128 us (0.962); the launches traced: 132 us -> 129 us
  waiting for transfers between devices: 52.1 us -> 46.1 us
  starting transfers between devices: 63.7 us -> 66 us
    ppermute x49, waiting for transfers between devices: 46.9 us -> 41.1 us  [exchange(): lax.ppermute(piece, 'dp', [(i, i ^ step[i % 2]) for i in range(devices)])]
    ppermute x49, starting transfers between devices: 59.4 us -> 61.3 us  [exchange(): lax.ppermute(piece, 'dp', [(i, i ^ step[i % 2]) for i in range(devices)])]
  transfers between devices with their start and end apart: 53 -> 53, of which waited for: 24 -> 22; matrix products, arithmetic and copies ran while one was open for 0% -> 0% of each run, Pallas kernels for 7% -> 7%
where the time goes in v1:
time: 128 us; the launch traced here: 129 us
  starting transfers between devices  66 us (52%)
  waiting for transfers between devices  46.1 us (36%)
  Pallas kernels  13.5 us (11%)
  between operations  1.35 us (1%)
    ppermute x49, starting transfers between devices, exchange(): lax.ppermute(piece, 'dp', [(i, i ^ step[i % 2]) for i in range(devices)])  61.3 us
    ppermute x49, waiting for transfers between devices, exchange(): lax.ppermute(piece, 'dp', [(i, i ^ step[i % 2]) for i in range(devices)])  41.1 us
    pallas_call x14, Pallas kernels, call(): pl.pallas_call(lambda *refs: kernel(*refs[:given], *refs[given + len(afte...  11.9 us
    ppermute x4, waiting for transfers between devices, across(): return lax.ppermute(array, 'dp', pairs)  4.97 us
    ppermute x4, starting transfers between devices, across(): return lax.ppermute(array, 'dp', pairs)  4.67 us
  transfers between devices with their start and end apart: 53, of which 22 were waited for; matrix products, arithmetic and copies ran while one was open for 0% of the time, Pallas kernels for 7%

profile of v1, /device:TPU:0, one launch (start us, length us, event | category | flops | bytes accessed | tf_op | source)
XLA Modules:
  0.0 128.8 jit_solution(18349648779932692520)
XLA Ops:
  0.6 1.1 copy-done
  1.8 3.0 %collective-permute-start.156 = (bf16[8,5120]{1,0:T(8,128)(2,1)S(1)}, bf16[8,5120]{1,0:T(8,128)(2,1)S(1)}, u32[]{:S(2)}, u32[]{:S(2)}) collective-permute-start(bf16[8,5120]{1,0:T(8,128)(2,1)S(1)} %get-tuple-element.399), channel_id=1, source_target_pairs={{0,2},{1,5},{2,0},{3,7},{4,6},{5,1},{6,4},{7,3},{8,10},{9,13},{10,... | collective-permute-start | bytes 245768 | tf_op jit(solution)/shard_map/ppermute | solution.py:342
  4.8 1.6 %collective-permute-start.157 = (bf16[8,5120]{1,0:T(8,128)(2,1)S(1)}, bf16[8,5120]{1,0:T(8,128)(2,1)S(1)}, u32[]{:S(2)}, u32[]{:S(2)}) collective-permute-start(bf16[8,5120]{1,0:T(8,128)(2,1)S(1)} %get-tuple-element.400), channel_id=1, source_target_pairs={{0,4},{1,3},{2,6},{3,1},{4,0},{5,7},{6,2},{7,5},{8,12},{9,11},{10,... | collective-permute-start | bytes 245768 | tf_op jit(solution)/shard_map/ppermute | solution.py:342
  6.9 1.2 collective-permute-start.160
  8.1 1.5 %collective-permute-start.161 = (bf16[8,5120]{1,0:T(8,128)(2,1)S(1)}, bf16[8,5120]{1,0:T(8,128)(2,1)S(1)}, u32[]{:S(2)}, u32[]{:S(2)}) collective-permute-start(bf16[8,5120]{1,0:T(8,128)(2,1)S(1)} %get-tuple-element.404), channel_id=1, source_target_pairs={{0,7},{1,6},{2,5},{3,4},{4,3},{5,2},{6,1},{7,0},{8,15},{9,14},{10,... | collective-permute-start | bytes 245768 | tf_op jit(solution)/shard_map/ppermute | solution.py:342
  10.1 1.1 collective-permute-start.162
  11.2 1.6 %shard_map.85 = (s32[5,8]{1,0:T(8,128)S(1)}, s32[1]{0:T(128)}) custom-call(s32[3,1,16]{2,1,0:T(1,128)} %bitcast.29, s32[16]{0:T(128)} %owner_ref.1), custom_call_target="tpu_custom_call" | custom-call | tf_op jit(solution)/shard_map/pallas_call | solution.py:144
  14.1 102.7 %conditional.2 = (bf16[128,5120]{1,0:T(8,128)(2,1)S(1)}, bf16[8,5120]{1,0:T(8,128)(2,1)S(1)}, bf16[8,5120]{1,0:T(8,128)(2,1)S(1)}, bf16[8,5120]{1,0:T(8,128)(2,1...) conditional(s32[]{:T(128)} %bitcast.5, (s32[5,8]{1,0:T(8,128)S(1)}, ...), branch_computations={%region_0.0_spmd, %region_1.0_spmd, %region_2.0_spmd, %region_3.0_... | conditional | flops 83886080 | bytes 39339764
  14.1 0.7 branch_1_fun.11.refs_1_
  14.8 2.7 %collective-permute-start.46 = (bf16[4,8,5120]{2,1,0:T(8,128)(2,1)S(1)}, bf16[4,8,5120]{2,1,0:T(8,128)(2,1)S(1)}, u32[]{:S(2)}, u32[]{:S(2)}) collective-permute-start(bf16[4,8,5120]{2,1,0:T(8,128)(2,1)S(1)} %branch_1_fun.11.refs_1_), channel_id=1, source_target_pairs={{0,8},{1,9},{2,10},{3,11},{4,12},{5,13},{6,14},{7,15},{8,0},{9,1},... | collective-permute-start | bytes 983048 | tf_op jit(solution)/shard_map/cond/branch_1_fun/ppermute | solution.py:317
  17.5 1.8 %collective-permute-start.39 = (bf16[8,5120]{1,0:T(8,128)(2,1)S(1)}, bf16[8,5120]{1,0:T(8,128)(2,1)S(1)}, u32[]{:S(2)}, u32[]{:S(2)}) collective-permute-start(bf16[8,5120]{1,0:T(8,128)(2,1)S(1)} %get-tuple-element.188), channel_id=1, source_target_pairs={{0,2},{1,5},{2,0},{3,7},{4,6},{5,1},{6,4},{7,3},{8,10},{9,13},{10,... | collective-permute-start | bytes 245768 | tf_op jit(solution)/shard_map/cond/branch_1_fun/ppermute | solution.py:342
  19.3 0.9 collective-permute-start.40
  20.1 0.9 collective-permute-start.41
  21.1 2.3 %collective-permute-done.39.refs_2_ = bf16[8,5120]{1,0:T(8,128)(2,1)S(1)} collective-permute-done((bf16[8,5120]{1,0:T(8,128)(2,1)S(1)}, bf16[8,5120]{1,0:T(8,128)(2,1)S(1)}, u32[]{:S(2)}, u32[]{:S(2)}) %collective-permute-start.39) | collective-permute-done | bytes 81952 | tf_op jit(solution)/shard_map/cond/branch_1_fun/ppermute | solution.py:342
  23.4 5.9 %collective-permute-start.43 = (bf16[8,5120]{1,0:T(8,128)(2,1)S(1)}, bf16[8,5120]{1,0:T(8,128)(2,1)S(1)}, u32[]{:S(2)}, u32[]{:S(2)}) collective-permute-start(bf16[8,5120]{1,0:T(8,128)(2,1)S(1)} %get-tuple-element.192), channel_id=1, source_target_pairs={{0,5},{1,2},{2,7},{3,0},{4,1},{5,6},{6,3},{7,4},{8,13},{9,10},{10,... | collective-permute-start | bytes 245768 | tf_op jit(solution)/shard_map/cond/branch_1_fun/ppermute | solution.py:342
  29.3 1.8 %collective-permute-start.45 = (bf16[8,5120]{1,0:T(8,128)(2,1)S(1)}, bf16[8,5120]{1,0:T(8,128)(2,1)S(1)}, u32[]{:S(2)}, u32[]{:S(2)}) collective-permute-start(bf16[8,5120]{1,0:T(8,128)(2,1)S(1)} %get-tuple-element.194), channel_id=1, source_target_pairs={{0,1},{1,0},{2,3},{3,2},{4,5},{5,4},{6,7},{7,6},{8,9},{9,8},{10,11... | collective-permute-start | bytes 245768 | tf_op jit(solution)/shard_map/cond/branch_1_fun/ppermute | solution.py:342
  31.3 3.7 %collective-permute-done.44.refs_7_ = bf16[8,5120]{1,0:T(8,128)(2,1)S(1)} collective-permute-done((bf16[8,5120]{1,0:T(8,128)(2,1)S(1)}, bf16[8,5120]{1,0:T(8,128)(2,1)S(1)}, u32[]{:S(2)}, u32[]{:S(2)}) %collective-permute-start.44) | collective-permute-done | bytes 81952 | tf_op jit(solution)/shard_map/cond/branch_1_fun/ppermute | solution.py:342
  35.1 0.7 branch_1_fun.13.refs_10_
  35.8 1.9 %collective-permute-start.47 = (bf16[4,8,5120]{2,1,0:T(8,128)(2,1)S(1)}, bf16[4,8,5120]{2,1,0:T(8,128)(2,1)S(1)}, u32[]{:S(2)}, u32[]{:S(2)}) collective-permute-start(bf16[4,8,5120]{2,1,0:T(8,128)(2,1)S(1)} %branch_1_fun.13.refs_10_), channel_id=1, source_target_pairs={{0,8},{1,9},{2,10},{3,11},{4,12},{5,13},{6,14},{7,15},{8,0},{9,1},... | collective-permute-start | bytes 983048 | tf_op jit(solution)/shard_map/cond/branch_1_fun/ppermute | solution.py:317
  37.7 0.7 branch_1_fun.14
  38.5 3.2 %collective-permute-start.49 = (bf16[8,5120]{1,0:T(8,128)(2,1)S(1)}, bf16[8,5120]{1,0:T(8,128)(2,1)S(1)}, u32[]{:S(2)}, u32[]{:S(2)}) collective-permute-start(bf16[8,5120]{1,0:T(8,128)(2,1)S(1)} %get-tuple-element.197), channel_id=1, source_target_pairs={{0,4},{1,3},{2,6},{3,1},{4,0},{5,7},{6,2},{7,5},{8,12},{9,11},{10,... | collective-permute-start | bytes 245768 | tf_op jit(solution)/shard_map/cond/branch_1_fun/ppermute | solution.py:342
  41.9 0.6 collective-permute-start.51
  42.6 0.8 collective-permute-done.48.refs_1_
  43.3 3.1 %collective-permute-start.52 = (bf16[8,5120]{1,0:T(8,128)(2,1)S(1)}, bf16[8,5120]{1,0:T(8,128)(2,1)S(1)}, u32[]{:S(2)}, u32[]{:S(2)}) collective-permute-start(bf16[8,5120]{1,0:T(8,128)(2,1)S(1)} %get-tuple-element.200), channel_id=1, source_target_pairs={{0,5},{1,2},{2,7},{3,0},{4,1},{5,6},{6,3},{7,4},{8,13},{9,10},{10,... | collective-permute-start | bytes 245768 | tf_op jit(solution)/shard_map/cond/branch_1_fun/ppermute | solution.py:342
  46.4 1.2 collective-permute-done.49.refs_2_
  47.6 1.1 collective-permute-start.53
  49.3 4.3 %collective-permute-done.51.refs_4_ = bf16[8,5120]{1,0:T(8,128)(2,1)S(1)} collective-permute-done((bf16[8,5120]{1,0:T(8,128)(2,1)S(1)}, bf16[8,5120]{1,0:T(8,128)(2,1)S(1)}, u32[]{:S(2)}, u32[]{:S(2)}) %collective-permute-start.51) | collective-permute-done | bytes 81952 | tf_op jit(solution)/shard_map/cond/branch_1_fun/ppermute | solution.py:342
  53.6 3.1 %collective-permute-done.53.refs_6_ = bf16[8,5120]{1,0:T(8,128)(2,1)S(1)} collective-permute-done((bf16[8,5120]{1,0:T(8,128)(2,1)S(1)}, bf16[8,5120]{1,0:T(8,128)(2,1)S(1)}, u32[]{:S(2)}, u32[]{:S(2)}) %collective-permute-start.53) | collective-permute-done | bytes 81952 | tf_op jit(solution)/shard_map/cond/branch_1_fun/ppermute | solution.py:342
  56.8 1.2 branch_1_fun.15
  58.0 0.8 branch_1_fun.16
  58.9 0.8 collective-permute-start.56
  59.7 2.6 %collective-permute-start.57 = (bf16[2,8,5120]{2,1,0:T(8,128)(2,1)S(1)}, bf16[2,8,5120]{2,1,0:T(8,128)(2,1)S(1)}, u32[]{:S(2)}, u32[]{:S(2)}) collective-permute-start(bf16[2,8,5120]{2,1,0:T(8,128)(2,1)S(1)} %get-tuple-element.209), channel_id=1, source_target_pairs={{0,6},{1,7},{2,4},{3,5},{4,2},{5,3},{6,0},{7,1},{8,14},{9,15},{10,... | collective-permute-start | bytes 491528 | tf_op jit(solution)/shard_map/cond/branch_1_fun/ppermute | solution.py:342
  62.3 1.7 %collective-permute-start.59 = (bf16[2,8,5120]{2,1,0:T(8,128)(2,1)S(1)}, bf16[2,8,5120]{2,1,0:T(8,128)(2,1)S(1)}, u32[]{:S(2)}, u32[]{:S(2)}) collective-permute-start(bf16[2,8,5120]{2,1,0:T(8,128)(2,1)S(1)} %get-tuple-element.211), channel_id=1, source_target_pairs={{0,5},{1,2},{2,7},{3,0},{4,1},{5,6},{6,3},{7,4},{8,13},{9,10},{10,... | collective-permute-start | bytes 491528 | tf_op jit(solution)/shard_map/cond/branch_1_fun/ppermute | solution.py:342
  64.1 3.8 %collective-permute-done.55.refs_2_.refs_1_ = bf16[2,8,5120]{2,1,0:T(8,128)(2,1)S(1)} collective-permute-done((bf16[2,8,5120]{2,1,0:T(8,128)(2,1)S(1)}, bf16[2,8,5120]{2,1,0:T(8,128)(2,1)S(1)}, u32[]{:S(2)}, u32[]{:S(2)}) %collective-permute-start.55) | collective-permute-done | bytes 163872 | tf_op jit(solution)/shard_map/cond/branch_1_fun/ppermute | solution.py:342
  67.9 2.6 %collective-permute-done.57.refs_4_.refs_3_ = bf16[2,8,5120]{2,1,0:T(8,128)(2,1)S(1)} collective-permute-done((bf16[2,8,5120]{2,1,0:T(8,128)(2,1)S(1)}, bf16[2,8,5120]{2,1,0:T(8,128)(2,1)S(1)}, u32[]{:S(2)}, u32[]{:S(2)}) %collective-permute-start.57) | collective-permute-done | bytes 163872 | tf_op jit(solution)/shard_map/cond/branch_1_fun/ppermute | solution.py:342
  70.5 1.7 %collective-permute-done.58.refs_5_.refs_4_ = bf16[2,8,5120]{2,1,0:T(8,128)(2,1)S(1)} collective-permute-done((bf16[2,8,5120]{2,1,0:T(8,128)(2,1)S(1)}, bf16[2,8,5120]{2,1,0:T(8,128)(2,1)S(1)}, u32[]{:S(2)}, u32[]{:S(2)}) %collective-permute-start.58) | collective-permute-done | bytes 163872 | tf_op jit(solution)/shard_map/cond/branch_1_fun/ppermute | solution.py:342
  72.2 3.6 %collective-permute-done.59.refs_6_.refs_5_ = bf16[2,8,5120]{2,1,0:T(8,128)(2,1)S(1)} collective-permute-done((bf16[2,8,5120]{2,1,0:T(8,128)(2,1)S(1)}, bf16[2,8,5120]{2,1,0:T(8,128)(2,1)S(1)}, u32[]{:S(2)}, u32[]{:S(2)}) %collective-permute-start.59) | collective-permute-done | bytes 163872 | tf_op jit(solution)/shard_map/cond/branch_1_fun/ppermute | solution.py:342
  75.9 0.8 branch_1_fun.17.refs_10_
  76.8 1.2 branch_1_fun.18
  78.0 1.4 %collective-permute-start.62 = (bf16[8,5120]{1,0:T(8,128)(2,1)S(1)}, bf16[8,5120]{1,0:T(8,128)(2,1)S(1)}, u32[]{:S(2)}, u32[]{:S(2)}) collective-permute-start(bf16[8,5120]{1,0:T(8,128)(2,1)S(1)} %get-tuple-element.217), channel_id=1, source_target_pairs={{0,2},{1,5},{2,0},{3,7},{4,6},{5,1},{6,4},{7,3},{8,10},{9,13},{10,... | collective-permute-start | bytes 245768 | tf_op jit(solution)/shard_map/cond/branch_1_fun/ppermute | solution.py:342
  79.5 0.9 collective-permute-start.63
  80.3 1.3 collective-permute-start.64
  81.9 1.1 collective-permute-done.62.refs_2_
  83.0 4.8 %collective-permute-start.66 = (bf16[8,5120]{1,0:T(8,128)(2,1)S(1)}, bf16[8,5120]{1,0:T(8,128)(2,1)S(1)}, u32[]{:S(2)}, u32[]{:S(2)}) collective-permute-start(bf16[8,5120]{1,0:T(8,128)(2,1)S(1)} %get-tuple-element.221), channel_id=1, source_target_pairs={{0,5},{1,2},{2,7},{3,0},{4,1},{5,6},{6,3},{7,4},{8,13},{9,10},{10,... | collective-permute-start | bytes 245768 | tf_op jit(solution)/shard_map/cond/branch_1_fun/ppermute | solution.py:342
  87.8 0.9 collective-permute-start.67
  88.7 1.2 collective-permute-start.68
  90.0 6.8 %collective-permute-done.67.refs_7_ = bf16[8,5120]{1,0:T(8,128)(2,1)S(1)} collective-permute-done((bf16[8,5120]{1,0:T(8,128)(2,1)S(1)}, bf16[8,5120]{1,0:T(8,128)(2,1)S(1)}, u32[]{:S(2)}, u32[]{:S(2)}) %collective-permute-start.67) | collective-permute-done | bytes 81952 | tf_op jit(solution)/shard_map/cond/branch_1_fun/ppermute | solution.py:342
  96.9 0.8 branch_1_fun.19.refs_10_
  97.8 1.0 branch_1_fun.21
  98.8 0.9 collective-permute-start.71
  99.6 1.7 %collective-permute-start.72 = (bf16[8,5120]{1,0:T(8,128)(2,1)S(1)}, bf16[8,5120]{1,0:T(8,128)(2,1)}, u32[]{:S(2)}, u32[]{:S(2)}) collective-permute-start(bf16[8,5120]{1,0:T(8,128)(2,1)S(1)} %get-tuple-element.234), channel_id=1, source_target_pairs={{0,4},{1,3},{2,6},{3,1},{4,0},{5,7},{6,2},{7,5},{8,12},{9,11},{10,... | collective-permute-start | bytes 245768 | tf_op jit(solution)/shard_map/cond/branch_1_fun/ppermute | solution.py:342
  101.4 0.9 collective-permute-start.73
  102.4 1.0 collective-permute-done.71
  103.4 6.5 %collective-permute-start.75 = (bf16[8,5120]{1,0:T(8,128)(2,1)S(1)}, bf16[8,5120]{1,0:T(8,128)(2,1)}, u32[]{:S(2)}, u32[]{:S(2)}) collective-permute-start(bf16[8,5120]{1,0:T(8,128)(2,1)S(1)} %get-tuple-element.237), channel_id=1, source_target_pairs={{0,5},{1,2},{2,7},{3,0},{4,1},{5,6},{6,3},{7,4},{8,13},{9,10},{10,... | collective-permute-start | bytes 245768 | tf_op jit(solution)/shard_map/cond/branch_1_fun/ppermute | solution.py:342
  109.8 5.0 %collective-permute-done.70.refs_9_ = bf16[4,8,5120]{2,1,0:T(8,128)(2,1)S(1)} collective-permute-done((bf16[4,8,5120]{2,1,0:T(8,128)(2,1)S(1)}, bf16[4,8,5120]{2,1,0:T(8,128)(2,1)S(1)}, u32[]{:S(2)}, u32[]{:S(2)}) %collective-permute-start.70) | collective-permute-done | bytes 327712 | tf_op jit(solution)/shard_map/cond/branch_1_fun/ppermute | solution.py:317
  115.3 1.0 branch_1_fun.20
  116.9 1.3 collective-permute-start.163
  118.1 2.3 %collective-permute-start.165 = (bf16[8,5120]{1,0:T(8,128)(2,1)S(1)}, bf16[8,5120]{1,0:T(8,128)(2,1)S(1)}, u32[]{:S(2)}, u32[]{:S(2)}) collective-permute-start(bf16[8,5120]{1,0:T(8,128)(2,1)S(1)} %get-tuple-element.410), channel_id=1, source_target_pairs={{0,6},{1,7},{2,4},{3,5},{4,2},{5,3},{6,0},{7,1},{8,14},{9,15},{10,... | collective-permute-start | bytes 245768 | tf_op jit(solution)/shard_map/ppermute | solution.py:342
  121.0 1.2 collective-permute-start.167
  122.2 0.7 collective-permute-start.168
  123.1 2.0 %shard_map.88 = bf16[8,8,5120]{2,1,0:T(8,128)(2,1)} custom-call(bf16[8,5120]{1,0:T(8,128)(2,1)S(1)} %get-tuple-element.415.refs_0_, bf16[8,5120]{1,0:T(8,128)(2,1)} %get-tuple-element.416.refs_1_, bf16[8,5120]{1,0:T(8,128)(2,1)} %get-tuple-element.417.refs_2_, bf16[8,5120]{1,0:T(8,128)(2,1)} %get-tuple-element.418.refs_3_, ...), custom_call_target="tpu_custom_call" | custom-call | tf_op jit(solution)/shard_map/pallas_call | solution.py:81
  125.2 1.0 collective-permute-done.167.refs_5_
  126.2 1.7 %collective-permute-done.168.refs_6_ = bf16[8,5120]{1,0:T(8,128)(2,1)S(1)} collective-permute-done((bf16[8,5120]{1,0:T(8,128)(2,1)S(1)}, bf16[8,5120]{1,0:T(8,128)(2,1)S(1)}, u32[]{:S(2)}, u32[]{:S(2)}) %collective-permute-start.168) | collective-permute-done | bytes 81952 | tf_op jit(solution)/shard_map/ppermute | solution.py:342
  127.9 0.9 shard_map.87
  (69 shorter events, 5.6 us)
Async XLA Ops:
  0.6 1.1 copy-start
  1.8 6.4 %collective-permute-start.156 = (bf16[8,5120]{1,0:T(8,128)(2,1)S(1)}, bf16[8,5120]{1,0:T(8,128)(2,1)S(1)}, u32[]{:S(2)}, u32[]{:S(2)}) collective-permute-start(bf16[8,5120]{1,0:T(8,128)(2,1)S(1)} %get-tuple-element.399), channel_id=1, source_target_pairs={{0,2},{1,5},{2,0},{3,7},{4,6},{5,1},{6,4},{7,3},{8,10},{9,13},{10,... | collective-permute-start | bytes 245768 | tf_op jit(solution)/shard_map/ppermute | solution.py:342
  4.8 5.3 %collective-permute-start.157 = (bf16[8,5120]{1,0:T(8,128)(2,1)S(1)}, bf16[8,5120]{1,0:T(8,128)(2,1)S(1)}, u32[]{:S(2)}, u32[]{:S(2)}) collective-permute-start(bf16[8,5120]{1,0:T(8,128)(2,1)S(1)} %get-tuple-element.400), channel_id=1, source_target_pairs={{0,4},{1,3},{2,6},{3,1},{4,0},{5,7},{6,2},{7,5},{8,12},{9,11},{10,... | collective-permute-start | bytes 245768 | tf_op jit(solution)/shard_map/ppermute | solution.py:342
  6.4 7.1 %collective-permute-start.158 = (bf16[8,5120]{1,0:T(8,128)(2,1)S(1)}, bf16[8,5120]{1,0:T(8,128)(2,1)S(1)}, u32[]{:S(2)}, u32[]{:S(2)}) collective-permute-start(bf16[8,5120]{1,0:T(8,128)(2,1)S(1)} %get-tuple-element.401), channel_id=1, source_target_pairs={{0,6},{1,7},{2,4},{3,5},{4,2},{5,3},{6,0},{7,1},{8,14},{9,15},{10,... | collective-permute-start | bytes 245768 | tf_op jit(solution)/shard_map/ppermute | solution.py:342
  6.4 7.1 %collective-permute-start.159 = (bf16[8,5120]{1,0:T(8,128)(2,1)S(1)}, bf16[8,5120]{1,0:T(8,128)(2,1)S(1)}, u32[]{:S(2)}, u32[]{:S(2)}) collective-permute-start(bf16[8,5120]{1,0:T(8,128)(2,1)S(1)} %get-tuple-element.402), channel_id=1, source_target_pairs={{0,3},{1,4},{2,1},{3,6},{4,7},{5,0},{6,5},{7,2},{8,11},{9,12},{10,... | collective-permute-start | bytes 245768 | tf_op jit(solution)/shard_map/ppermute | solution.py:342
  6.9 6.6 %collective-permute-start.160 = (bf16[8,5120]{1,0:T(8,128)(2,1)S(1)}, bf16[8,5120]{1,0:T(8,128)(2,1)S(1)}, u32[]{:S(2)}, u32[]{:S(2)}) collective-permute-start(bf16[8,5120]{1,0:T(8,128)(2,1)S(1)} %get-tuple-element.403), channel_id=1, source_target_pairs={{0,5},{1,2},{2,7},{3,0},{4,1},{5,6},{6,3},{7,4},{8,13},{9,10},{10,... | collective-permute-start | bytes 245768 | tf_op jit(solution)/shard_map/ppermute | solution.py:342
  8.1 6.0 %collective-permute-start.161 = (bf16[8,5120]{1,0:T(8,128)(2,1)S(1)}, bf16[8,5120]{1,0:T(8,128)(2,1)S(1)}, u32[]{:S(2)}, u32[]{:S(2)}) collective-permute-start(bf16[8,5120]{1,0:T(8,128)(2,1)S(1)} %get-tuple-element.404), channel_id=1, source_target_pairs={{0,7},{1,6},{2,5},{3,4},{4,3},{5,2},{6,1},{7,0},{8,15},{9,14},{10,... | collective-permute-start | bytes 245768 | tf_op jit(solution)/shard_map/ppermute | solution.py:342
  10.1 4.0 %collective-permute-start.162 = (bf16[8,5120]{1,0:T(8,128)(2,1)S(1)}, bf16[8,5120]{1,0:T(8,128)(2,1)S(1)}, u32[]{:S(2)}, u32[]{:S(2)}) collective-permute-start(bf16[8,5120]{1,0:T(8,128)(2,1)S(1)} %get-tuple-element.405), channel_id=1, source_target_pairs={{0,1},{1,0},{2,3},{3,2},{4,5},{5,4},{6,7},{7,6},{8,9},{9,8},{10,11... | collective-permute-start | bytes 245768 | tf_op jit(solution)/shard_map/ppermute | solution.py:342
  14.1 3.4 %copy-start.10 = (bf16[8,8,5120]{2,1,0:T(8,128)(2,1)S(1)}, bf16[8,8,5120]{2,1,0:T(8,128)(2,1)}, u32[]{:S(2)}) copy-start(bf16[8,8,5120]{2,1,0:T(8,128)(2,1)} %get-tuple-element.178.refs_0_) | copy-start | bytes 1966084 | tf_op jit(solution)/shard_map/conditional
  14.8 20.3 %collective-permute-start.46 = (bf16[4,8,5120]{2,1,0:T(8,128)(2,1)S(1)}, bf16[4,8,5120]{2,1,0:T(8,128)(2,1)S(1)}, u32[]{:S(2)}, u32[]{:S(2)}) collective-permute-start(bf16[4,8,5120]{2,1,0:T(8,128)(2,1)S(1)} %branch_1_fun.11.refs_1_), channel_id=1, source_target_pairs={{0,8},{1,9},{2,10},{3,11},{4,12},{5,13},{6,14},{7,15},{8,0},{9,1},... | collective-permute-start | bytes 983048 | tf_op jit(solution)/shard_map/cond/branch_1_fun/ppermute | solution.py:317
  17.5 5.9 %collective-permute-start.39 = (bf16[8,5120]{1,0:T(8,128)(2,1)S(1)}, bf16[8,5120]{1,0:T(8,128)(2,1)S(1)}, u32[]{:S(2)}, u32[]{:S(2)}) collective-permute-start(bf16[8,5120]{1,0:T(8,128)(2,1)S(1)} %get-tuple-element.188), channel_id=1, source_target_pairs={{0,2},{1,5},{2,0},{3,7},{4,6},{5,1},{6,4},{7,3},{8,10},{9,13},{10,... | collective-permute-start | bytes 245768 | tf_op jit(solution)/shard_map/cond/branch_1_fun/ppermute | solution.py:342
  19.3 10.0 %collective-permute-start.40 = (bf16[8,5120]{1,0:T(8,128)(2,1)S(1)}, bf16[8,5120]{1,0:T(8,128)(2,1)S(1)}, u32[]{:S(2)}, u32[]{:S(2)}) collective-permute-start(bf16[8,5120]{1,0:T(8,128)(2,1)S(1)} %get-tuple-element.189), channel_id=1, source_target_pairs={{0,4},{1,3},{2,6},{3,1},{4,0},{5,7},{6,2},{7,5},{8,12},{9,11},{10,... | collective-permute-start | bytes 245768 | tf_op jit(solution)/shard_map/cond/branch_1_fun/ppermute | solution.py:342
  20.1 9.1 %collective-permute-start.41 = (bf16[8,5120]{1,0:T(8,128)(2,1)S(1)}, bf16[8,5120]{1,0:T(8,128)(2,1)S(1)}, u32[]{:S(2)}, u32[]{:S(2)}) collective-permute-start(bf16[8,5120]{1,0:T(8,128)(2,1)S(1)} %get-tuple-element.190), channel_id=1, source_target_pairs={{0,6},{1,7},{2,4},{3,5},{4,2},{5,3},{6,0},{7,1},{8,14},{9,15},{10,... | collective-permute-start | bytes 245768 | tf_op jit(solution)/shard_map/cond/branch_1_fun/ppermute | solution.py:342
  21.1 10.0 %collective-permute-start.42 = (bf16[8,5120]{1,0:T(8,128)(2,1)S(1)}, bf16[8,5120]{1,0:T(8,128)(2,1)S(1)}, u32[]{:S(2)}, u32[]{:S(2)}) collective-permute-start(bf16[8,5120]{1,0:T(8,128)(2,1)S(1)} %get-tuple-element.191), channel_id=1, source_target_pairs={{0,3},{1,4},{2,1},{3,6},{4,7},{5,0},{6,5},{7,2},{8,11},{9,12},{10,... | collective-permute-start | bytes 245768 | tf_op jit(solution)/shard_map/cond/branch_1_fun/ppermute | solution.py:342
  23.4 7.9 %collective-permute-start.43 = (bf16[8,5120]{1,0:T(8,128)(2,1)S(1)}, bf16[8,5120]{1,0:T(8,128)(2,1)S(1)}, u32[]{:S(2)}, u32[]{:S(2)}) collective-permute-start(bf16[8,5120]{1,0:T(8,128)(2,1)S(1)} %get-tuple-element.192), channel_id=1, source_target_pairs={{0,5},{1,2},{2,7},{3,0},{4,1},{5,6},{6,3},{7,4},{8,13},{9,10},{10,... | collective-permute-start | bytes 245768 | tf_op jit(solution)/shard_map/cond/branch_1_fun/ppermute | solution.py:342
  29.3 5.8 %collective-permute-start.44 = (bf16[8,5120]{1,0:T(8,128)(2,1)S(1)}, bf16[8,5120]{1,0:T(8,128)(2,1)S(1)}, u32[]{:S(2)}, u32[]{:S(2)}) collective-permute-start(bf16[8,5120]{1,0:T(8,128)(2,1)S(1)} %get-tuple-element.193), channel_id=1, source_target_pairs={{0,7},{1,6},{2,5},{3,4},{4,3},{5,2},{6,1},{7,0},{8,15},{9,14},{10,... | collective-permute-start | bytes 245768 | tf_op jit(solution)/shard_map/cond/branch_1_fun/ppermute | solution.py:342
  29.3 5.8 %collective-permute-start.45 = (bf16[8,5120]{1,0:T(8,128)(2,1)S(1)}, bf16[8,5120]{1,0:T(8,128)(2,1)S(1)}, u32[]{:S(2)}, u32[]{:S(2)}) collective-permute-start(bf16[8,5120]{1,0:T(8,128)(2,1)S(1)} %get-tuple-element.194), channel_id=1, source_target_pairs={{0,1},{1,0},{2,3},{3,2},{4,5},{5,4},{6,7},{7,6},{8,9},{9,8},{10,11... | collective-permute-start | bytes 245768 | tf_op jit(solution)/shard_map/cond/branch_1_fun/ppermute | solution.py:342
  35.1 21.7 %copy-start.2 = (bf16[128,5120]{1,0:T(8,128)(2,1)S(1)}, bf16[128,5120]{1,0:T(8,128)(2,1)}, u32[]{:S(2)}) copy-start(bf16[128,5120]{1,0:T(8,128)(2,1)} %get-tuple-element.203.refs_8_.refs_9_) | copy-start | bytes 3932164 | tf_op jit(solution)/shard_map/conditional
  35.1 21.7 %copy-start.6 = (bf16[128,5120]{1,0:T(8,128)(2,1)S(1)}, bf16[128,5120]{1,0:T(8,128)(2,1)}, u32[]{:S(2)}) copy-start(bf16[128,5120]{1,0:T(8,128)(2,1)} %get-tuple-element.204.refs_9_.refs_8_) | copy-start | bytes 3932164 | tf_op jit(solution)/shard_map/conditional
  35.8 22.2 %collective-permute-start.47 = (bf16[4,8,5120]{2,1,0:T(8,128)(2,1)S(1)}, bf16[4,8,5120]{2,1,0:T(8,128)(2,1)S(1)}, u32[]{:S(2)}, u32[]{:S(2)}) collective-permute-start(bf16[4,8,5120]{2,1,0:T(8,128)(2,1)S(1)} %branch_1_fun.13.refs_10_), channel_id=1, source_target_pairs={{0,8},{1,9},{2,10},{3,11},{4,12},{5,13},{6,14},{7,15},{8,0},{9,1},... | collective-permute-start | bytes 983048 | tf_op jit(solution)/shard_map/cond/branch_1_fun/ppermute | solution.py:317
  38.4 5.0 %collective-permute-start.48 = (bf16[8,5120]{1,0:T(8,128)(2,1)S(1)}, bf16[8,5120]{1,0:T(8,128)(2,1)S(1)}, u32[]{:S(2)}, u32[]{:S(2)}) collective-permute-start(bf16[8,5120]{1,0:T(8,128)(2,1)S(1)} %get-tuple-element.196), channel_id=1, source_target_pairs={{0,2},{1,5},{2,0},{3,7},{4,6},{5,1},{6,4},{7,3},{8,10},{9,13},{10,... | collective-permute-start | bytes 245768 | tf_op jit(solution)/shard_map/cond/branch_1_fun/ppermute | solution.py:342
  38.5 9.2 %collective-permute-start.49 = (bf16[8,5120]{1,0:T(8,128)(2,1)S(1)}, bf16[8,5120]{1,0:T(8,128)(2,1)S(1)}, u32[]{:S(2)}, u32[]{:S(2)}) collective-permute-start(bf16[8,5120]{1,0:T(8,128)(2,1)S(1)} %get-tuple-element.197), channel_id=1, source_target_pairs={{0,4},{1,3},{2,6},{3,1},{4,0},{5,7},{6,2},{7,5},{8,12},{9,11},{10,... | collective-permute-start | bytes 245768 | tf_op jit(solution)/shard_map/cond/branch_1_fun/ppermute | solution.py:342
  41.6 7.1 %collective-permute-start.50 = (bf16[8,5120]{1,0:T(8,128)(2,1)S(1)}, bf16[8,5120]{1,0:T(8,128)(2,1)S(1)}, u32[]{:S(2)}, u32[]{:S(2)}) collective-permute-start(bf16[8,5120]{1,0:T(8,128)(2,1)S(1)} %get-tuple-element.198), channel_id=1, source_target_pairs={{0,6},{1,7},{2,4},{3,5},{4,2},{5,3},{6,0},{7,1},{8,14},{9,15},{10,... | collective-permute-start | bytes 245768 | tf_op jit(solution)/shard_map/cond/branch_1_fun/ppermute | solution.py:342
  41.9 11.7 %collective-permute-start.51 = (bf16[8,5120]{1,0:T(8,128)(2,1)S(1)}, bf16[8,5120]{1,0:T(8,128)(2,1)S(1)}, u32[]{:S(2)}, u32[]{:S(2)}) collective-permute-start(bf16[8,5120]{1,0:T(8,128)(2,1)S(1)} %get-tuple-element.199), channel_id=1, source_target_pairs={{0,3},{1,4},{2,1},{3,6},{4,7},{5,0},{6,5},{7,2},{8,11},{9,12},{10,... | collective-permute-start | bytes 245768 | tf_op jit(solution)/shard_map/cond/branch_1_fun/ppermute | solution.py:342
  43.3 10.3 %collective-permute-start.52 = (bf16[8,5120]{1,0:T(8,128)(2,1)S(1)}, bf16[8,5120]{1,0:T(8,128)(2,1)S(1)}, u32[]{:S(2)}, u32[]{:S(2)}) collective-permute-start(bf16[8,5120]{1,0:T(8,128)(2,1)S(1)} %get-tuple-element.200), channel_id=1, source_target_pairs={{0,5},{1,2},{2,7},{3,0},{4,1},{5,6},{6,3},{7,4},{8,13},{9,10},{10,... | collective-permute-start | bytes 245768 | tf_op jit(solution)/shard_map/cond/branch_1_fun/ppermute | solution.py:342
  47.6 9.1 %collective-permute-start.53 = (bf16[8,5120]{1,0:T(8,128)(2,1)S(1)}, bf16[8,5120]{1,0:T(8,128)(2,1)S(1)}, u32[]{:S(2)}, u32[]{:S(2)}) collective-permute-start(bf16[8,5120]{1,0:T(8,128)(2,1)S(1)} %get-tuple-element.201), channel_id=1, source_target_pairs={{0,7},{1,6},{2,5},{3,4},{4,3},{5,2},{6,1},{7,0},{8,15},{9,14},{10,... | collective-permute-start | bytes 245768 | tf_op jit(solution)/shard_map/cond/branch_1_fun/ppermute | solution.py:342
  48.7 8.0 %collective-permute-start.54 = (bf16[8,5120]{1,0:T(8,128)(2,1)S(1)}, bf16[8,5120]{1,0:T(8,128)(2,1)S(1)}, u32[]{:S(2)}, u32[]{:S(2)}) collective-permute-start(bf16[8,5120]{1,0:T(8,128)(2,1)S(1)} %get-tuple-element.202), channel_id=1, source_target_pairs={{0,1},{1,0},{2,3},{3,2},{4,5},{5,4},{6,7},{7,6},{8,9},{9,8},{10,11... | collective-permute-start | bytes 245768 | tf_op jit(solution)/shard_map/cond/branch_1_fun/ppermute | solution.py:342
  58.7 9.1 %collective-permute-start.55 = (bf16[2,8,5120]{2,1,0:T(8,128)(2,1)S(1)}, bf16[2,8,5120]{2,1,0:T(8,128)(2,1)S(1)}, u32[]{:S(2)}, u32[]{:S(2)}) collective-permute-start(bf16[2,8,5120]{2,1,0:T(8,128)(2,1)S(1)} %get-tuple-element.207), channel_id=1, source_target_pairs={{0,2},{1,5},{2,0},{3,7},{4,6},{5,1},{6,4},{7,3},{8,10},{9,13},{10,... | collective-permute-start | bytes 491528 | tf_op jit(solution)/shard_map/cond/branch_1_fun/ppermute | solution.py:342
  58.9 9.0 %collective-permute-start.56 = (bf16[2,8,5120]{2,1,0:T(8,128)(2,1)S(1)}, bf16[2,8,5120]{2,1,0:T(8,128)(2,1)S(1)}, u32[]{:S(2)}, u32[]{:S(2)}) collective-permute-start(bf16[2,8,5120]{2,1,0:T(8,128)(2,1)S(1)} %get-tuple-element.208), channel_id=1, source_target_pairs={{0,4},{1,3},{2,6},{3,1},{4,0},{5,7},{6,2},{7,5},{8,12},{9,11},{10,... | collective-permute-start | bytes 491528 | tf_op jit(solution)/shard_map/cond/branch_1_fun/ppermute | solution.py:342
  59.7 10.8 %collective-permute-start.57 = (bf16[2,8,5120]{2,1,0:T(8,128)(2,1)S(1)}, bf16[2,8,5120]{2,1,0:T(8,128)(2,1)S(1)}, u32[]{:S(2)}, u32[]{:S(2)}) collective-permute-start(bf16[2,8,5120]{2,1,0:T(8,128)(2,1)S(1)} %get-tuple-element.209), channel_id=1, source_target_pairs={{0,6},{1,7},{2,4},{3,5},{4,2},{5,3},{6,0},{7,1},{8,14},{9,15},{10,... | collective-permute-start | bytes 491528 | tf_op jit(solution)/shard_map/cond/branch_1_fun/ppermute | solution.py:342
  62.3 9.9 %collective-permute-start.58 = (bf16[2,8,5120]{2,1,0:T(8,128)(2,1)S(1)}, bf16[2,8,5120]{2,1,0:T(8,128)(2,1)S(1)}, u32[]{:S(2)}, u32[]{:S(2)}) collective-permute-start(bf16[2,8,5120]{2,1,0:T(8,128)(2,1)S(1)} %get-tuple-element.210), channel_id=1, source_target_pairs={{0,3},{1,4},{2,1},{3,6},{4,7},{5,0},{6,5},{7,2},{8,11},{9,12},{10,... | collective-permute-start | bytes 491528 | tf_op jit(solution)/shard_map/cond/branch_1_fun/ppermute | solution.py:342
  62.3 13.5 %collective-permute-start.59 = (bf16[2,8,5120]{2,1,0:T(8,128)(2,1)S(1)}, bf16[2,8,5120]{2,1,0:T(8,128)(2,1)S(1)}, u32[]{:S(2)}, u32[]{:S(2)}) collective-permute-start(bf16[2,8,5120]{2,1,0:T(8,128)(2,1)S(1)} %get-tuple-element.211), channel_id=1, source_target_pairs={{0,5},{1,2},{2,7},{3,0},{4,1},{5,6},{6,3},{7,4},{8,13},{9,10},{10,... | collective-permute-start | bytes 491528 | tf_op jit(solution)/shard_map/cond/branch_1_fun/ppermute | solution.py:342
  67.9 8.0 %collective-permute-start.60 = (bf16[2,8,5120]{2,1,0:T(8,128)(2,1)S(1)}, bf16[2,8,5120]{2,1,0:T(8,128)(2,1)S(1)}, u32[]{:S(2)}, u32[]{:S(2)}) collective-permute-start(bf16[2,8,5120]{2,1,0:T(8,128)(2,1)S(1)} %get-tuple-element.212), channel_id=1, source_target_pairs={{0,7},{1,6},{2,5},{3,4},{4,3},{5,2},{6,1},{7,0},{8,15},{9,14},{10,... | collective-permute-start | bytes 491528 | tf_op jit(solution)/shard_map/cond/branch_1_fun/ppermute | solution.py:342
  67.9 8.0 %collective-permute-start.61 = (bf16[2,8,5120]{2,1,0:T(8,128)(2,1)S(1)}, bf16[2,8,5120]{2,1,0:T(8,128)(2,1)S(1)}, u32[]{:S(2)}, u32[]{:S(2)}) collective-permute-start(bf16[2,8,5120]{2,1,0:T(8,128)(2,1)S(1)} %get-tuple-element.213), channel_id=1, source_target_pairs={{0,1},{1,0},{2,3},{3,2},{4,5},{5,4},{6,7},{7,6},{8,9},{9,8},{10,11... | collective-permute-start | bytes 491528 | tf_op jit(solution)/shard_map/cond/branch_1_fun/ppermute | solution.py:342
  76.7 20.1 %collective-permute-start.69 = (bf16[4,8,5120]{2,1,0:T(8,128)(2,1)S(1)}, bf16[4,8,5120]{2,1,0:T(8,128)(2,1)S(1)}, u32[]{:S(2)}, u32[]{:S(2)}) collective-permute-start(bf16[4,8,5120]{2,1,0:T(8,128)(2,1)S(1)} %branch_1_fun.17.refs_10_), channel_id=1, source_target_pairs={{0,8},{1,9},{2,10},{3,11},{4,12},{5,13},{6,14},{7,15},{8,0},{9,1},... | collective-permute-start | bytes 983048 | tf_op jit(solution)/shard_map/cond/branch_1_fun/ppermute | solution.py:317
  78.0 5.0 %collective-permute-start.62 = (bf16[8,5120]{1,0:T(8,128)(2,1)S(1)}, bf16[8,5120]{1,0:T(8,128)(2,1)S(1)}, u32[]{:S(2)}, u32[]{:S(2)}) collective-permute-start(bf16[8,5120]{1,0:T(8,128)(2,1)S(1)} %get-tuple-element.217), channel_id=1, source_target_pairs={{0,2},{1,5},{2,0},{3,7},{4,6},{5,1},{6,4},{7,3},{8,10},{9,13},{10,... | collective-permute-start | bytes 245768 | tf_op jit(solution)/shard_map/cond/branch_1_fun/ppermute | solution.py:342
  79.5 8.4 %collective-permute-start.63 = (bf16[8,5120]{1,0:T(8,128)(2,1)S(1)}, bf16[8,5120]{1,0:T(8,128)(2,1)S(1)}, u32[]{:S(2)}, u32[]{:S(2)}) collective-permute-start(bf16[8,5120]{1,0:T(8,128)(2,1)S(1)} %get-tuple-element.218), channel_id=1, source_target_pairs={{0,4},{1,3},{2,6},{3,1},{4,0},{5,7},{6,2},{7,5},{8,12},{9,11},{10,... | collective-permute-start | bytes 245768 | tf_op jit(solution)/shard_map/cond/branch_1_fun/ppermute | solution.py:342
  80.3 8.4 %collective-permute-start.64 = (bf16[8,5120]{1,0:T(8,128)(2,1)S(1)}, bf16[8,5120]{1,0:T(8,128)(2,1)S(1)}, u32[]{:S(2)}, u32[]{:S(2)}) collective-permute-start(bf16[8,5120]{1,0:T(8,128)(2,1)S(1)} %get-tuple-element.219), channel_id=1, source_target_pairs={{0,6},{1,7},{2,4},{3,5},{4,2},{5,3},{6,0},{7,1},{8,14},{9,15},{10,... | collective-permute-start | bytes 245768 | tf_op jit(solution)/shard_map/cond/branch_1_fun/ppermute | solution.py:342
  81.6 8.4 %collective-permute-start.65 = (bf16[8,5120]{1,0:T(8,128)(2,1)S(1)}, bf16[8,5120]{1,0:T(8,128)(2,1)S(1)}, u32[]{:S(2)}, u32[]{:S(2)}) collective-permute-start(bf16[8,5120]{1,0:T(8,128)(2,1)S(1)} %get-tuple-element.220), channel_id=1, source_target_pairs={{0,3},{1,4},{2,1},{3,6},{4,7},{5,0},{6,5},{7,2},{8,11},{9,12},{10,... | collective-permute-start | bytes 245768 | tf_op jit(solution)/shard_map/cond/branch_1_fun/ppermute | solution.py:342
  83.0 7.0 %collective-permute-start.66 = (bf16[8,5120]{1,0:T(8,128)(2,1)S(1)}, bf16[8,5120]{1,0:T(8,128)(2,1)S(1)}, u32[]{:S(2)}, u32[]{:S(2)}) collective-permute-start(bf16[8,5120]{1,0:T(8,128)(2,1)S(1)} %get-tuple-element.221), channel_id=1, source_target_pairs={{0,5},{1,2},{2,7},{3,0},{4,1},{5,6},{6,3},{7,4},{8,13},{9,10},{10,... | collective-permute-start | bytes 245768 | tf_op jit(solution)/shard_map/cond/branch_1_fun/ppermute | solution.py:342
  87.8 9.0 %collective-permute-start.67 = (bf16[8,5120]{1,0:T(8,128)(2,1)S(1)}, bf16[8,5120]{1,0:T(8,128)(2,1)S(1)}, u32[]{:S(2)}, u32[]{:S(2)}) collective-permute-start(bf16[8,5120]{1,0:T(8,128)(2,1)S(1)} %get-tuple-element.222), channel_id=1, source_target_pairs={{0,7},{1,6},{2,5},{3,4},{4,3},{5,2},{6,1},{7,0},{8,15},{9,14},{10,... | collective-permute-start | bytes 245768 | tf_op jit(solution)/shard_map/cond/branch_1_fun/ppermute | solution.py:342
  88.7 8.1 %collective-permute-start.68 = (bf16[8,5120]{1,0:T(8,128)(2,1)S(1)}, bf16[8,5120]{1,0:T(8,128)(2,1)S(1)}, u32[]{:S(2)}, u32[]{:S(2)}) collective-permute-start(bf16[8,5120]{1,0:T(8,128)(2,1)S(1)} %get-tuple-element.223), channel_id=1, source_target_pairs={{0,1},{1,0},{2,3},{3,2},{4,5},{5,4},{6,7},{7,6},{8,9},{9,8},{10,11... | collective-permute-start | bytes 245768 | tf_op jit(solution)/shard_map/cond/branch_1_fun/ppermute | solution.py:342
  97.7 17.1 %collective-permute-start.70 = (bf16[4,8,5120]{2,1,0:T(8,128)(2,1)S(1)}, bf16[4,8,5120]{2,1,0:T(8,128)(2,1)S(1)}, u32[]{:S(2)}, u32[]{:S(2)}) collective-permute-start(bf16[4,8,5120]{2,1,0:T(8,128)(2,1)S(1)} %branch_1_fun.19.refs_10_), channel_id=1, source_target_pairs={{0,8},{1,9},{2,10},{3,11},{4,12},{5,13},{6,14},{7,15},{8,0},{9,1},... | collective-permute-start | bytes 983048 | tf_op jit(solution)/shard_map/cond/branch_1_fun/ppermute | solution.py:317
  98.8 4.6 %collective-permute-start.71 = (bf16[8,5120]{1,0:T(8,128)(2,1)S(1)}, bf16[8,5120]{1,0:T(8,128)(2,1)}, u32[]{:S(2)}, u32[]{:S(2)}) collective-permute-start(bf16[8,5120]{1,0:T(8,128)(2,1)S(1)} %get-tuple-element.233), channel_id=1, source_target_pairs={{0,2},{1,5},{2,0},{3,7},{4,6},{5,1},{6,4},{7,3},{8,10},{9,13},{10,... | collective-permute-start | bytes 245768 | tf_op jit(solution)/shard_map/cond/branch_1_fun/ppermute | solution.py:342
  99.6 10.2 %collective-permute-start.72 = (bf16[8,5120]{1,0:T(8,128)(2,1)S(1)}, bf16[8,5120]{1,0:T(8,128)(2,1)}, u32[]{:S(2)}, u32[]{:S(2)}) collective-permute-start(bf16[8,5120]{1,0:T(8,128)(2,1)S(1)} %get-tuple-element.234), channel_id=1, source_target_pairs={{0,4},{1,3},{2,6},{3,1},{4,0},{5,7},{6,2},{7,5},{8,12},{9,11},{10,... | collective-permute-start | bytes 245768 | tf_op jit(solution)/shard_map/cond/branch_1_fun/ppermute | solution.py:342
  101.4 14.9 %collective-permute-start.73 = (bf16[8,5120]{1,0:T(8,128)(2,1)S(1)}, bf16[8,5120]{1,0:T(8,128)(2,1)}, u32[]{:S(2)}, u32[]{:S(2)}) collective-permute-start(bf16[8,5120]{1,0:T(8,128)(2,1)S(1)} %get-tuple-element.235), channel_id=1, source_target_pairs={{0,6},{1,7},{2,4},{3,5},{4,2},{5,3},{6,0},{7,1},{8,14},{9,15},{10,... | collective-permute-start | bytes 245768 | tf_op jit(solution)/shard_map/cond/branch_1_fun/ppermute | solution.py:342
  102.3 14.0 %collective-permute-start.74 = (bf16[8,5120]{1,0:T(8,128)(2,1)S(1)}, bf16[8,5120]{1,0:T(8,128)(2,1)}, u32[]{:S(2)}, u32[]{:S(2)}) collective-permute-start(bf16[8,5120]{1,0:T(8,128)(2,1)S(1)} %get-tuple-element.236), channel_id=1, source_target_pairs={{0,3},{1,4},{2,1},{3,6},{4,7},{5,0},{6,5},{7,2},{8,11},{9,12},{10,... | collective-permute-start | bytes 245768 | tf_op jit(solution)/shard_map/cond/branch_1_fun/ppermute | solution.py:342
  103.4 12.9 %collective-permute-start.75 = (bf16[8,5120]{1,0:T(8,128)(2,1)S(1)}, bf16[8,5120]{1,0:T(8,128)(2,1)}, u32[]{:S(2)}, u32[]{:S(2)}) collective-permute-start(bf16[8,5120]{1,0:T(8,128)(2,1)S(1)} %get-tuple-element.237), channel_id=1, source_target_pairs={{0,5},{1,2},{2,7},{3,0},{4,1},{5,6},{6,3},{7,4},{8,13},{9,10},{10,... | collective-permute-start | bytes 245768 | tf_op jit(solution)/shard_map/cond/branch_1_fun/ppermute | solution.py:342
  109.8 7.0 %collective-permute-start.76 = (bf16[8,5120]{1,0:T(8,128)(2,1)S(1)}, bf16[8,5120]{1,0:T(8,128)(2,1)}, u32[]{:S(2)}, u32[]{:S(2)}) collective-permute-start(bf16[8,5120]{1,0:T(8,128)(2,1)S(1)} %get-tuple-element.238), channel_id=1, source_target_pairs={{0,7},{1,6},{2,5},{3,4},{4,3},{5,2},{6,1},{7,0},{8,15},{9,14},{10,... | collective-permute-start | bytes 245768 | tf_op jit(solution)/shard_map/cond/branch_1_fun/ppermute | solution.py:342
  114.8 2.0 %collective-permute-start.77 = (bf16[8,5120]{1,0:T(8,128)(2,1)S(1)}, bf16[8,5120]{1,0:T(8,128)(2,1)}, u32[]{:S(2)}, u32[]{:S(2)}) collective-permute-start(bf16[8,5120]{1,0:T(8,128)(2,1)S(1)} %get-tuple-element.239), channel_id=1, source_target_pairs={{0,1},{1,0},{2,3},{3,2},{4,5},{5,4},{6,7},{7,6},{8,9},{9,8},{10,11... | collective-permute-start | bytes 245768 | tf_op jit(solution)/shard_map/cond/branch_1_fun/ppermute | solution.py:342
  116.8 11.9 %copy-start.13 = (bf16[128,5120]{1,0:T(8,128)(2,1)}, bf16[128,5120]{1,0:T(8,128)(2,1)S(1)}, u32[]{:S(2)}) copy-start(bf16[128,5120]{1,0:T(8,128)(2,1)S(1)} %get-tuple-element.406) | copy-start | bytes 3932164
  116.9 5.3 %collective-permute-start.163 = (bf16[8,5120]{1,0:T(8,128)(2,1)S(1)}, bf16[8,5120]{1,0:T(8,128)(2,1)S(1)}, u32[]{:S(2)}, u32[]{:S(2)}) collective-permute-start(bf16[8,5120]{1,0:T(8,128)(2,1)S(1)} %get-tuple-element.408), channel_id=1, source_target_pairs={{0,2},{1,5},{2,0},{3,7},{4,6},{5,1},{6,4},{7,3},{8,10},{9,13},{10,... | collective-permute-start | bytes 245768 | tf_op jit(solution)/shard_map/ppermute | solution.py:342
  118.1 4.9 %collective-permute-start.164 = (bf16[8,5120]{1,0:T(8,128)(2,1)S(1)}, bf16[8,5120]{1,0:T(8,128)(2,1)S(1)}, u32[]{:S(2)}, u32[]{:S(2)}) collective-permute-start(bf16[8,5120]{1,0:T(8,128)(2,1)S(1)} %get-tuple-element.409), channel_id=1, source_target_pairs={{0,4},{1,3},{2,6},{3,1},{4,0},{5,7},{6,2},{7,5},{8,12},{9,11},{10,... | collective-permute-start | bytes 245768 | tf_op jit(solution)/shard_map/ppermute | solution.py:342
  118.1 7.0 %collective-permute-start.165 = (bf16[8,5120]{1,0:T(8,128)(2,1)S(1)}, bf16[8,5120]{1,0:T(8,128)(2,1)S(1)}, u32[]{:S(2)}, u32[]{:S(2)}) collective-permute-start(bf16[8,5120]{1,0:T(8,128)(2,1)S(1)} %get-tuple-element.410), channel_id=1, source_target_pairs={{0,6},{1,7},{2,4},{3,5},{4,2},{5,3},{6,0},{7,1},{8,14},{9,15},{10,... | collective-permute-start | bytes 245768 | tf_op jit(solution)/shard_map/ppermute | solution.py:342
  120.4 4.8 %collective-permute-start.166 = (bf16[8,5120]{1,0:T(8,128)(2,1)S(1)}, bf16[8,5120]{1,0:T(8,128)(2,1)S(1)}, u32[]{:S(2)}, u32[]{:S(2)}) collective-permute-start(bf16[8,5120]{1,0:T(8,128)(2,1)S(1)} %get-tuple-element.411), channel_id=1, source_target_pairs={{0,3},{1,4},{2,1},{3,6},{4,7},{5,0},{6,5},{7,2},{8,11},{9,12},{10,... | collective-permute-start | bytes 245768 | tf_op jit(solution)/shard_map/ppermute | solution.py:342
  121.0 5.2 %collective-permute-start.167 = (bf16[8,5120]{1,0:T(8,128)(2,1)S(1)}, bf16[8,5120]{1,0:T(8,128)(2,1)S(1)}, u32[]{:S(2)}, u32[]{:S(2)}) collective-permute-start(bf16[8,5120]{1,0:T(8,128)(2,1)S(1)} %get-tuple-element.412), channel_id=1, source_target_pairs={{0,5},{1,2},{2,7},{3,0},{4,1},{5,6},{6,3},{7,4},{8,13},{9,10},{10,... | collective-permute-start | bytes 245768 | tf_op jit(solution)/shard_map/ppermute | solution.py:342
  122.2 5.7 %collective-permute-start.168 = (bf16[8,5120]{1,0:T(8,128)(2,1)S(1)}, bf16[8,5120]{1,0:T(8,128)(2,1)S(1)}, u32[]{:S(2)}, u32[]{:S(2)}) collective-permute-start(bf16[8,5120]{1,0:T(8,128)(2,1)S(1)} %get-tuple-element.413), channel_id=1, source_target_pairs={{0,7},{1,6},{2,5},{3,4},{4,3},{5,2},{6,1},{7,0},{8,15},{9,14},{10,... | collective-permute-start | bytes 245768 | tf_op jit(solution)/shard_map/ppermute | solution.py:342
  123.1 4.8 %collective-permute-start.169 = (bf16[8,5120]{1,0:T(8,128)(2,1)S(1)}, bf16[8,5120]{1,0:T(8,128)(2,1)S(1)}, u32[]{:S(2)}, u32[]{:S(2)}) collective-permute-start(bf16[8,5120]{1,0:T(8,128)(2,1)S(1)} %get-tuple-element.414), channel_id=1, source_target_pairs={{0,1},{1,0},{2,3},{3,2},{4,5},{5,4},{6,7},{7,6},{8,9},{9,8},{10,11... | collective-permute-start | bytes 245768 | tf_op jit(solution)/shard_map/ppermute | solution.py:342
